TPU v7x, 512 devices: a whole 4x8x8 slice. The times are simulated.
512 devices in a mesh: flap: 16 (over z_lo, y), gust: 16 (over x, z_hi), span: 2 (over core).
Axes of the slice: x: 4, y: 8, z: 8 (z_hi: 4, z_lo: 2; z = z_hi * 2 + z_lo), core: 2. Of those that a mesh axis runs over, the one named last changes fastest.
Arguments:
- state: float32 [16, 16, 5, 4, 48, 128], P('flap', 'gust', None, 'span'), may hold values from -1 to 4, as said below
- frame_velocity: float32 [16, 16, 3], P('flap', 'gust'), may hold values from -3 to 3
- dtau: float32 [4, 48, 128], P('span'), may hold values from 0.02 to 0.08
- live_mask: int32 [4, 48, 128], P('span'), may hold values 0 or 1
- link: int32 [128], replicated, may hold values from 0 to 127, each once
Outputs:
- state_out: float32 [16, 16, 5, 4, 48, 128], P('flap', 'gust', None, 'span')
Inputs may be any that keep to these rules, and one draw needn't show every extreme that they name: `state`: every cell holds a density of 0.7 or more, and a total energy that leaves a pressure of 0.5 or more.
All inputs are finite; a program needn't handle non-finite values. No bound on the sum of `live_mask` on one device may be relied on, other than what follows from the above.
Results may differ from a plain program's by a relative error of at most 0.0003.
Values sent between devices are 32-bit elements; how exact they have to be, the bound alone decides.
No kernel may reach another device: no remote copies, remote signals or barrier semaphores. Data moves between devices by JAX's collectives and lax.ppermute only.
A program may use at most 64 MiB of HBM per device.

v0:
```python
import jax
import jax.numpy as jnp
from jax import lax
from jax.sharding import PartitionSpec as P

STEPS = 2


GAMMA = 1.4
VISC = 0.12


def extended_2(cells, sides, width):
    for axis, dim in sides:
        count = lax.axis_size(axis)
        ends = count - 1
        head = lax.slice_in_dim(cells, 0, width, axis=dim)
        tail = lax.slice_in_dim(cells, cells.shape[dim] - width, cells.shape[dim], axis=dim)
        cells = jnp.concatenate(
            [
                lax.ppermute(tail, axis, [(i, (i + 1) % count) for i in range(ends)]),
                cells,
                lax.ppermute(head, axis, [((i + 1) % count, i) for i in range(ends)]),
            ],
            axis=dim,
        )
    return cells


def instance_matrix(count, omega):
    rows = jnp.arange(count)[:, None]
    cols = jnp.arange(count)[None, :]
    offset = rows - cols
    angle = jnp.pi * offset.astype(jnp.float32) / count
    parity = jnp.where(offset % 2 == 0, 1.0, -1.0).astype(jnp.float32)
    offdiag = offset != 0
    safe = jnp.where(offdiag, angle, 0.5 * jnp.pi)
    first = jnp.where(offdiag, 0.5 * parity / jnp.tan(safe), 0.0)
    sines = jnp.sin(safe)
    second = jnp.where(
        offdiag, -0.5 * parity / (sines * sines), -(count * count / 12.0 + 1.0 / 6.0)
    )
    return omega * first - VISC * second


def unit_vector(axis, ndim):
    values = jnp.array([1.0 if a == axis else 0.0 for a in range(3)], jnp.float32)
    return values.reshape((3,) + (1,) * ndim)


def primitives(state):
    density = state[0]
    velocity = state[1:4] / density
    pressure = (GAMMA - 1.0) * (state[4] - 0.5 * density * jnp.sum(velocity * velocity, axis=0))
    return (density, velocity, pressure)


def speed_fix(value, sound):
    magnitude = jnp.abs(value)
    delta = 0.1 * sound
    return jnp.where(magnitude < delta, (value * value + delta * delta) / (2.0 * delta), magnitude)


def roe_flux(left, right, axis, grid_speed):
    normal = unit_vector(axis, left.ndim - 1)
    rho_l, vel_l, p_l = primitives(left)
    rho_r, vel_r, p_r = primitives(right)
    enth_l = (left[4] + p_l) / rho_l
    enth_r = (right[4] + p_r) / rho_r
    flux_l = (vel_l[axis] - grid_speed) * left + jnp.concatenate(
        [jnp.zeros_like(p_l)[None], p_l[None] * normal, (p_l * vel_l[axis])[None]], 0
    )
    flux_r = (vel_r[axis] - grid_speed) * right + jnp.concatenate(
        [jnp.zeros_like(p_r)[None], p_r[None] * normal, (p_r * vel_r[axis])[None]], 0
    )
    ratio = jnp.sqrt(rho_r / rho_l)
    weight_l = 1.0 / (1.0 + ratio)
    weight_r = ratio / (1.0 + ratio)
    vel_t = weight_l * vel_l + weight_r * vel_r
    enth_t = weight_l * enth_l + weight_r * enth_r
    speed_sq = jnp.sum(vel_t * vel_t, axis=0)
    sound_sq = (GAMMA - 1.0) * (enth_t - 0.5 * speed_sq)
    sound = jnp.sqrt(sound_sq)
    rho_t = jnp.sqrt(rho_l * rho_r)
    normal_t = vel_t[axis]
    jump_p = p_r - p_l
    jump_rho = rho_r - rho_l
    jump_vel = vel_r - vel_l
    jump_n = jump_vel[axis]
    alpha_one = (jump_p - rho_t * sound * jump_n) / (2.0 * sound_sq)
    alpha_three = (jump_p + rho_t * sound * jump_n) / (2.0 * sound_sq)
    alpha_two = jump_rho - jump_p / sound_sq
    lam_one = speed_fix(normal_t - grid_speed - sound, sound)
    lam_two = speed_fix(normal_t - grid_speed, sound)
    lam_three = speed_fix(normal_t - grid_speed + sound, sound)
    ones = jnp.ones_like(sound)[None]
    wave_one = jnp.concatenate([ones, vel_t - sound * normal, (enth_t - normal_t * sound)[None]], 0)
    wave_two = jnp.concatenate([ones, vel_t, (0.5 * speed_sq)[None]], 0)
    wave_three = jnp.concatenate(
        [ones, vel_t + sound * normal, (enth_t + normal_t * sound)[None]], 0
    )
    shear = jnp.concatenate(
        [
            jnp.zeros_like(sound)[None],
            jump_vel - jump_n * normal,
            (jnp.sum(vel_t * jump_vel, axis=0) - normal_t * jump_n)[None],
        ],
        0,
    )
    dissip = (
        lam_one * alpha_one * wave_one
        + lam_two * (alpha_two * wave_two + rho_t * shear)
        + lam_three * alpha_three * wave_three
    )
    return 0.5 * (flux_l + flux_r) - 0.5 * dissip


def reflect(state, axis):
    return jnp.concatenate([state[: 1 + axis], -state[1 + axis : 2 + axis], state[2 + axis :]], 0)


def face_pair(left, right, mask_left, mask_right, axis):
    left_state = jnp.where(mask_left > 0, left, reflect(right, axis))
    right_state = jnp.where(mask_right > 0, right, reflect(left, axis))
    return (left_state, right_state)


def divergence(padded, live_mask, link, grid_velocity):
    state = padded[:, 1:-1]
    span_flux = roe_flux(padded[:, :-1], padded[:, 1:], 2, grid_velocity[2])
    total = span_flux[:, 1:] - span_flux[:, :-1]
    ahead = jnp.roll(state, -1, axis=3)
    mask_ahead = jnp.roll(live_mask, -1, axis=2)
    left_i, right_i = face_pair(state, ahead, live_mask, mask_ahead, 0)
    chord_flux = roe_flux(left_i, right_i, 0, grid_velocity[0])
    total = total + chord_flux - jnp.roll(chord_flux, 1, axis=3)
    below = jnp.take(state[:, :, 0, :], link, axis=2)[:, :, None]
    mask_below = jnp.take(live_mask[:, 0, :], link, axis=1)[:, None]
    extended = jnp.concatenate([below, state, state[:, :, -1:]], axis=2)
    mask_ext = jnp.concatenate([mask_below, live_mask, jnp.ones_like(live_mask[:, -1:])], axis=1)
    left_j, right_j = face_pair(
        extended[:, :, :-1], extended[:, :, 1:], mask_ext[:, :-1], mask_ext[:, 1:], 1
    )
    normal_flux = roe_flux(left_j, right_j, 1, grid_velocity[1])
    return total + normal_flux[:, :, 1:] - normal_flux[:, :, :-1]


def span_padded(field):
    padded = extended_2(field, (("span", 1),), 1)
    position = lax.axis_index("span")
    count = lax.axis_size("span")
    lower = jnp.where(position == 0, field[:, :1], padded[:, :1])
    upper = jnp.where(position == count - 1, field[:, -1:], padded[:, -1:])
    return jnp.concatenate([lower, padded[:, 1:-1], upper], axis=1)


def time_terms(flat, flap_matrix, gust_matrix):
    flap_row = lax.dynamic_index_in_dim(flap_matrix, lax.axis_index("flap"), 0, keepdims=False)
    gust_row = lax.dynamic_index_in_dim(gust_matrix, lax.axis_index("gust"), 0, keepdims=False)
    weights = flap_row
    flap_part = jnp.einsum(
        "a,abcx->bcx",
        weights,
        lax.all_gather(flat, "flap", axis=0, tiled=True),
        precision=lax.Precision.HIGHEST,
    )[None]
    weights = gust_row
    gust_part = jnp.einsum(
        "b,abcx->acx",
        weights,
        lax.all_gather(flat, "gust", axis=1, tiled=True),
        precision=lax.Precision.HIGHEST,
    )[:, None]
    return flap_part + gust_part


def shards(state, frame_velocity, dtau, live_mask, link):
    flap_matrix = instance_matrix(lax.axis_size("flap"), 0.8)
    gust_matrix = instance_matrix(lax.axis_size("gust"), 1.2944)
    grid_velocity = frame_velocity[0, 0]
    field = state[0, 0]
    for step in range(STEPS):
        spatial = divergence(span_padded(field), live_mask, link, grid_velocity)
        flat = field.reshape((1, 1, 5, -1))
        temporal = time_terms(flat, flap_matrix, gust_matrix).reshape(field.shape)
        residual = spatial + temporal
        field = jnp.where(live_mask > 0, field - dtau * residual, field)
    return field[None, None]


def solution(mesh):
    in_specs = (
        P("flap", "gust", None, "span", None, None),
        P("flap", "gust", None),
        P("span", None, None),
        P("span", None, None),
        P(),
    )
    out_specs = P("flap", "gust", None, "span", None, None)
    return jax.shard_map(shards, mesh=mesh, in_specs=in_specs, out_specs=out_specs, check_vma=False)
```

profile of v0, /device:TPU:2, one launch (start us, length us, event | category | flops | bytes accessed | tf_op | source)
XLA Modules:
  0.0 354.3 jit_solution(9208161498879016095)
XLA Ops:
  7.3 1.7 fusion.313
  9.0 2.4 collective-permute-start
  22.0 1.7 fusion.128
  29.2 2.4 copy.2710
  31.6 2.2 copy.2542
  33.8 2.4 copy.2709
  36.1 2.2 copy.2530
  38.3 2.4 copy.2712
  40.7 2.2 copy.2572
  57.7 39.0 %all-gather.7.cloned.1.call-done = f32[1,16,5,12288]{3,0,2,1:T(1,128)} async-done(((f32[1,1,5,12288]{3,0,2,1:T(1,128)}), f32[1,16,5,12288]{3,0,2,1:T(1,128)}) %all-gather.7.cloned.1.call-update) | async-done | bytes 3932176 | tf_op jit(solution)/shard_map/all_gather | solution.py:171
  96.7 6.1 %fusion.4 = f32[1,5,12288]{2,0,1:T(1,128)S(1)} fusion(f32[1,16,5,12288]{3,0,2,1:T(1,128)} %all-gather.7.cloned.1.call-done, f32[16,16]{1,0:T(8,128)S(1)} %get-tuple-element.289, s32[]{:T(128)S(6)} %select_n.211, f32[16,16]{1,0:T(8,128)S(1)} %get-tuple-element.288), kind=kOutput, calls=%fused_computation.7 | convolution fusion | flops 11796512 | bytes 4178948 | tf_op jit(solution)/shard_map/b,abcx->acx/dot_general | solution.py:168
  102.9 72.5 %all-gather.5.cloned.1.call-done = f32[16,1,5,12288]{3,1,2,0:T(1,128)} async-done(((f32[1,1,5,12288]{3,1,2,0:T(1,128)}), f32[16,1,5,12288]{3,1,2,0:T(1,128)}) %all-gather.5.cloned.1.call-update) | async-done | bytes 3932176 | tf_op jit(solution)/shard_map/all_gather | solution.py:164
  175.4 6.1 %fusion.6 = f32[1,5,12288]{2,0,1:T(1,128)S(1)} fusion(f32[16,1,5,12288]{3,1,2,0:T(1,128)} %all-gather.5.cloned.1.call-done, f32[16,16]{1,0:T(8,128)S(1)} %get-tuple-element.289, s32[]{:T(128)S(6)} %select_n.210, f32[16,16]{1,0:T(8,128)S(1)} %get-tuple-element.288), kind=kOutput, calls=%fused_computation.9 | convolution fusion | flops 11796512 | bytes 4178948 | tf_op jit(solution)/shard_map/a,abcx->bcx/dot_general | solution.py:161
  183.0 1.8 slice.628
  193.9 1.7 copy.2722
  195.5 2.2 copy.2617
  200.4 2.2 copy.2605
  202.6 3.1 copy.2724
  205.7 2.8 copy.2647
  209.3 1.9 collective-permute-start.2
  225.8 36.2 %all-gather.11.cloned.1.call-done = f32[1,16,5,12288]{3,0,2,1:T(1,128)} async-done(((f32[1,1,5,12288]{3,0,2,1:T(1,128)}), f32[1,16,5,12288]{3,0,2,1:T(1,128)}) %all-gather.11.cloned.1.call-update) | async-done | bytes 3932176 | tf_op jit(solution)/shard_map/all_gather | solution.py:171
  261.9 6.1 %fusion = f32[1,5,12288]{2,0,1:T(1,128)S(1)} fusion(f32[1,16,5,12288]{3,0,2,1:T(1,128)} %all-gather.11.cloned.1.call-done, f32[16,16]{1,0:T(8,128)} %copy-done.43, s32[]{:T(128)S(6)} %select_n.211, f32[16,16]{1,0:T(8,128)S(1)} %get-tuple-element.288), kind=kOutput, calls=%fused_computation.3 | convolution fusion | flops 11796512 | bytes 4178948 | tf_op jit(solution)/shard_map/b,abcx->acx/dot_general | solution.py:168
  268.0 72.3 %all-gather.9.cloned.1.call-done = f32[16,1,5,12288]{3,1,2,0:T(1,128)} async-done(((f32[1,1,5,12288]{3,1,2,0:T(1,128)}), f32[16,1,5,12288]{3,1,2,0:T(1,128)}) %all-gather.9.cloned.1.call-update) | async-done | bytes 3932176 | tf_op jit(solution)/shard_map/all_gather | solution.py:164
  340.4 6.1 %fusion.2 = f32[1,5,12288]{2,0,1:T(1,128)S(1)} fusion(f32[16,1,5,12288]{3,1,2,0:T(1,128)} %all-gather.9.cloned.1.call-done, f32[16,16]{1,0:T(8,128)} %copy-done.43, s32[]{:T(128)S(6)} %select_n.210, f32[16,16]{1,0:T(8,128)S(1)} %get-tuple-element.288), kind=kOutput, calls=%fused_computation.5 | convolution fusion | flops 11796512 | bytes 4178948 | tf_op jit(solution)/shard_map/a,abcx->bcx/dot_general | solution.py:161
  (243 shorter events, 60.3 us)
Async XLA Ops:
  6.5 17.2 %copy-start.2 = (f32[1,1,5,2,48,128]{5,4,3,2,1,0:T(8,128)S(1)}, f32[1,1,5,2,48,128]{5,4,3,2,1,0:T(8,128)}, u32[]{:S(2)}) copy-start(f32[1,1,5,2,48,128]{5,4,3,2,1,0:T(8,128)} %param.15) | copy-start | bytes 737284
  6.5 18.8 %copy-start.20 = (s32[2,48,128]{2,1,0:T(8,128)S(1)}, s32[2,48,128]{2,1,0:T(8,128)}, u32[]{:S(2)}) copy-start(s32[2,48,128]{2,1,0:T(8,128)} %param.18) | copy-start | bytes 147460
  6.5 18.9 %copy-start.47 = (f32[1,1,3]{2,1,0:T(1,128)S(1)}, f32[1,1,3]{2,1,0:T(1,128)}, u32[]{:S(2)}) copy-start(f32[1,1,3]{2,1,0:T(1,128)} %param.16) | copy-start | bytes 40
  6.5 90.2 %all-gather.7.cloned.1.call-start = ((), (), s32[]{:S(2)}) async-start(), calls=%async_computation.1 | async-start | bytes 4177920 | tf_op jit(solution)/shard_map/all_gather | solution.py:171
  7.3 168.1 %all-gather.5.cloned.1.call-start = ((), (), s32[]{:S(2)}) async-start(), calls=%async_computation | async-start | bytes 4177920 | tf_op jit(solution)/shard_map/all_gather | solution.py:164
  9.0 44.6 %collective-permute-start = (f32[5,1,48,128]{3,2,1,0:T(8,128)}, f32[5,1,48,128]{3,2,1,0:T(8,128)}, u32[]{:S(2)}, u32[]{:S(2)}) collective-permute-start(f32[5,1,48,128]{3,2,1,0:T(8,128)} %get-tuple-element.163), channel_id=1, source_target_pairs={{0,1},{2,3},{4,5},{6,7},{8,9},{10,11},{12,13},{14,15},{16,17},{18,... | collective-permute-start | bytes 368648 | tf_op jit(solution)/shard_map/ppermute | solution.py:21
  11.4 42.2 %collective-permute-start.1 = (f32[5,1,48,128]{3,2,1,0:T(8,128)}, f32[5,1,48,128]{3,2,1,0:T(8,128)}, u32[]{:S(2)}, u32[]{:S(2)}) collective-permute-start(f32[5,1,48,128]{3,2,1,0:T(8,128)} %get-tuple-element.164), channel_id=1, source_target_pairs={{1,0},{3,2},{5,4},{7,6},{9,8},{11,10},{13,12},{15,14},{17,16},{19,... | collective-permute-start | bytes 368648 | tf_op jit(solution)/shard_map/ppermute | solution.py:23
  12.7 249.2 %all-gather.11.cloned.1.call-start = ((), (), s32[]{:S(2)}) async-start(), calls=%async_computation.3 | async-start | bytes 4177920 | tf_op jit(solution)/shard_map/all_gather | solution.py:171
  14.9 14.3 %copy-start.45 = (pred[128]{0:T(512)(128)(4,1)}, pred[128]{0:T(512)(128)(4,1)S(1)}, u32[]{:S(2)}) copy-start(pred[128]{0:T(512)(128)(4,1)S(1)} %compare_and_fusion) | copy-start | bytes 388
  15.0 14.1 %copy-start.44 = (s32[1024]{0:T(1024)}, s32[1024]{0:T(1024)S(1)}, u32[]{:S(2)}) copy-start(s32[1024]{0:T(1024)S(1)} %pad_clamp_fusion) | copy-start | bytes 12292
  42.9 14.4 %copy-start.41 = (f32[5]{0:T(128)}, f32[5]{0:T(128)S(1)}, u32[]{:S(2)}) copy-start(f32[5]{0:T(128)S(1)} %pad.156.clone) | copy-start | bytes 64
  43.1 9.0 %copy-start.49 = (f32[3]{0:T(128)S(1)}, f32[3]{0:T(128)}, u32[]{:S(2)}) copy-start(f32[3]{0:T(128)} %constant.138.clone) | copy-start | bytes 40
  53.6 121.8 %copy-start.43 = (f32[16,16]{1,0:T(8,128)}, f32[16,16]{1,0:T(8,128)S(1)}, u32[]{:S(2)}) copy-start(f32[16,16]{1,0:T(8,128)S(1)} %get-tuple-element.289) | copy-start | bytes 3076
  96.7 85.1 %copy-start.33 = (f32[2,48,128]{2,1,0:T(8,128)S(1)}, f32[2,48,128]{2,1,0:T(8,128)}, u32[]{:S(2)}) copy-start(f32[2,48,128]{2,1,0:T(8,128)} %param.17) | copy-start | bytes 147460
  102.8 85.5 %copy-start.46 = (pred[128]{0:T(512)(128)(4,1)S(1)}, pred[128]{0:T(512)(128)(4,1)}, u32[]{:S(2)}) copy-start(pred[128]{0:T(512)(128)(4,1)} %copy-done.45) | copy-start | bytes 388
  181.5 8.9 %copy-start.36 = (pred[2,49,128]{2,1,0:T(8,128)(4,1)S(1)}, pred[2,49,128]{2,1,0:T(8,128)(4,1)}, u32[]{:S(2)}) copy-start(pred[2,49,128]{2,1,0:T(8,128)(4,1)} %copy-done.35) | copy-start | bytes 37636
  182.8 157.6 %all-gather.9.cloned.1.call-start = ((), (), s32[]{:S(2)}) async-start(), calls=%async_computation.2 | async-start | bytes 4177920 | tf_op jit(solution)/shard_map/all_gather | solution.py:164
  202.6 10.0 %copy-start.3 = (f32[5,2,48,127]{3,2,1,0:T(8,128)S(1)}, f32[5,2,48,127]{3,2,1,0:T(8,128)}, u32[]{:S(2)}) copy-start(f32[5,2,48,127]{3,2,1,0:T(8,128)} %slice.628) | copy-start | bytes 731524
  202.6 10.3 %copy-start.1 = (f32[5,2,48,128]{3,2,1,0:T(8,128)S(1)}, f32[5,2,48,128]{3,2,1,0:T(8,128)}, u32[]{:S(2)}) copy-start(f32[5,2,48,128]{3,2,1,0:T(8,128)} %subtract_select_fusion.1) | copy-start | bytes 737284
  202.6 10.3 %copy-start.21 = (f32[3,2,48,128]{3,2,1,0:T(8,128)S(1)}, f32[3,2,48,128]{3,2,1,0:T(8,128)}, u32[]{:S(2)}) copy-start(f32[3,2,48,128]{3,2,1,0:T(8,128)} %slice.642) | copy-start | bytes 442372
  202.6 10.3 %copy-start.40 = (pred[2,48,128]{2,1,0:T(8,128)(4,1)S(1)}, pred[2,48,128]{2,1,0:T(8,128)(4,1)}, u32[]{:S(2)}) copy-start(pred[2,48,128]{2,1,0:T(8,128)(4,1)} %copy-done.39) | copy-start | bytes 36868
  209.3 12.3 %collective-permute-start.2 = (f32[5,1,48,128]{3,2,1,0:T(8,128)}, f32[5,1,48,128]{3,2,1,0:T(8,128)}, u32[]{:S(2)}, u32[]{:S(2)}) collective-permute-start(f32[5,1,48,128]{3,2,1,0:T(8,128)} %get-tuple-element.145), channel_id=1, source_target_pairs={{0,1},{2,3},{4,5},{6,7},{8,9},{10,11},{12,13},{14,15},{16,17},{18,... | collective-permute-start | bytes 368648 | tf_op jit(solution)/shard_map/ppermute | solution.py:21
  211.3 10.4 %collective-permute-start.3 = (f32[5,1,48,128]{3,2,1,0:T(8,128)}, f32[5,1,48,128]{3,2,1,0:T(8,128)}, u32[]{:S(2)}, u32[]{:S(2)}) collective-permute-start(f32[5,1,48,128]{3,2,1,0:T(8,128)} %get-tuple-element.146), channel_id=1, source_target_pairs={{1,0},{3,2},{5,4},{7,6},{9,8},{11,10},{13,12},{15,14},{17,16},{19,... | collective-permute-start | bytes 368648 | tf_op jit(solution)/shard_map/ppermute | solution.py:23
  225.8 121.1 %copy-start.34 = (f32[2,48,128]{2,1,0:T(8,128)S(1)}, f32[2,48,128]{2,1,0:T(8,128)}, u32[]{:S(2)}) copy-start(f32[2,48,128]{2,1,0:T(8,128)} %param.17) | copy-start | bytes 147460
  (37 other events, 174.9 us)
Sparse Core Ops, SparseCore 0:
  10.4 86.2 all-gather.6
  98.8 76.5 all-gather.4
  182.9 78.9 all-gather.10
  263.9 76.4 all-gather.8
where the time goes:
time: 356 us; the launch traced here: 354 us
  waiting for transfers between devices  221 us (62%)
  other arithmetic  44.2 us (12%)
  local copies, waits for them, and re-layouts  43.3 us (12%)
  matrix products  24.4 us (7%)
  between operations  14.4 us (4%)
  starting transfers between devices  7.23 us (2%)
    all_gather x2, waiting for transfers between devices, time_terms(): lax.all_gather(flat, 'flap', axis=0, tiled=True)  145 us
    all_gather x2, waiting for transfers between devices, time_terms(): lax.all_gather(flat, 'gust', axis=1, tiled=True)  75.2 us
    unnamed x117, local copies, waits for them, and re-layouts  15.8 us
    dot_general x2, matrix products, time_terms(): jnp.einsum('b,abcx->acx', weights, lax.all_gather(flat, 'gust', axis=1, t...  12.2 us
    dot_general x2, matrix products, time_terms(): jnp.einsum('a,abcx->bcx', weights, lax.all_gather(flat, 'flap', axis=0, t...  12.2 us
    reduce_sum x4, local copies, waits for them, and re-layouts, primitives(): jnp.sum(velocity * velocity, axis=0)  8.76 us
  transfers between devices with their start and end apart: 8, of which 4 were waited for; matrix products, arithmetic and copies ran while one was open for 27% of the time, Pallas kernels for 0%

commit v1 on v0

v1 whole, which is shorter than its diff:
```python
import functools
import math

import jax
import jax.numpy as jnp
import numpy as np
from jax import lax
from jax.experimental import pallas as pl
from jax.experimental.pallas import tpu as pltpu
from jax.sharding import PartitionSpec as P

VISC = 0.12
FLAP_OMEGA = 0.8
GUST_OMEGA = 1.2944

RHO, U, V, W, PR, EN, RT, LIVE = range(8)
PAD = 8


def instance_matrix(count, omega):
    offset = np.arange(count)[:, None] - np.arange(count)[None, :]
    angle = np.pi * offset / count
    parity = np.where(offset % 2 == 0, 1.0, -1.0)
    off = offset != 0
    safe = np.where(off, angle, 0.5 * np.pi)
    first = np.where(off, 0.5 * parity / np.tan(safe), 0.0)
    second = np.where(off, -0.5 * parity / np.sin(safe) ** 2, -(count * count / 12.0 + 1.0 / 6.0))
    return omega * first - VISC * second


def primitives(rho, m1, m2, m3, energy):
    inv = 1.0 / rho
    u, v, w = m1 * inv, m2 * inv, m3 * inv
    p = 0.4 * (energy - 0.5 * (m1 * u + m2 * v + m3 * w))
    return (rho, u, v, w, p, (energy + p) * inv, jnp.sqrt(jnp.abs(rho)))


def physical(cell, axis, g):
    rho, vel, p, enth = cell[RHO], cell[U : W + 1], cell[PR], cell[EN]
    mass = rho * (vel[axis] - g)
    mom = [mass * vel[a] + p if a == axis else mass * vel[a] for a in range(3)]
    return [mass, *mom, mass * enth + g * p]


def roe(left, right, axis, g):
    rho_l, vel_l, p_l, h_l, s_l = left[RHO], left[U : W + 1], left[PR], left[EN], left[RT]
    rho_r, vel_r, p_r, h_r, s_r = right[RHO], right[U : W + 1], right[PR], right[EN], right[RT]
    t1, t2 = [a for a in range(3) if a != axis]
    weight = s_r / (s_l + s_r)
    jump = [vel_r[a] - vel_l[a] for a in range(3)]
    vel = [vel_l[a] + weight * jump[a] for a in range(3)]
    enth = h_l + weight * (h_r - h_l)
    half_sq = 0.5 * (vel[0] * vel[0] + vel[1] * vel[1] + vel[2] * vel[2])
    c_sq = 0.4 * (enth - half_sq)
    inv_c = lax.rsqrt(c_sq)
    c = c_sq * inv_c
    delta = 0.1 * c
    scale = 5.0 * inv_c
    half_inv_sq = 0.5 * (inv_c * inv_c)
    rho_t = s_l * s_r
    dp = p_r - p_l
    drho = rho_r - rho_l
    swing = rho_t * c * jump[axis]

    def speed(value):
        size = jnp.abs(value)
        return jnp.where(size < delta, (value * value + delta * delta) * scale, size)

    rel = vel[axis] - g
    l2 = speed(rel)
    w1 = speed(rel - c) * ((dp - swing) * half_inv_sq)
    w3 = speed(rel + c) * ((dp + swing) * half_inv_sq)
    w2 = l2 * (drho - dp * (2.0 * half_inv_sq))
    shear = l2 * rho_t
    acoustic = w1 + w3
    total = acoustic + w2
    skew = (w3 - w1) * c
    mass_l = rho_l * (vel_l[axis] - g)
    mass_r = rho_r * (vel_r[axis] - g)
    out = [0.5 * (mass_l + mass_r - total)]
    for a in range(3):
        flux = mass_l * vel_l[a] + mass_r * vel_r[a]
        if a == axis:
            flux = flux + (p_l + p_r) - (total * vel[a] + skew)
        else:
            flux = flux - (total * vel[a] + shear * jump[a])
        out.append(0.5 * flux)
    loss = acoustic * enth + w2 * half_sq + skew * vel[axis]
    loss = loss + shear * (vel[t1] * jump[t1] + vel[t2] * jump[t2])
    out.append(0.5 * (mass_l * h_l + mass_r * h_r + g * (p_l + p_r) - loss))
    return out


def walled(left, right, axis):
    live_l, live_r = left[LIVE] > 0.0, right[LIVE] > 0.0
    n = U + axis
    new_l, new_r = [], []
    for f in range(LIVE):
        if f == n:
            new_l.append(jnp.where(live_l, left[f], -right[f]))
            new_r.append(jnp.where(live_r, right[f], -left[f]))
        else:
            new_l.append(jnp.where(live_l, left[f], right[f]))
            new_r.append(jnp.where(live_r, right[f], left[f]))
    return new_l, new_r


def divergence_blocks(load, halo_ref, mask_ref, link_ref, speed_ref, first, cells, faces, emit):
    nj = mask_ref.shape[1]
    blocks = nj // 8
    g0, g1, g2 = speed_ref[0], speed_ref[1], speed_ref[2]
    first = first > 0

    def rows(b):
        return pl.multiple_of(8 * b, 8)

    def fill(b, carry):
        row = rows(b)
        for k in range(2):
            values = primitives(*[load(f, k, row) for f in range(5)])
            for f, value in enumerate(values):
                cells[f, k, pl.ds(PAD + row, 8), :] = value
            live = jnp.where(mask_ref[k, pl.ds(row, 8), :] > 0, 1.0, 0.0)
            cells[LIVE, k, pl.ds(PAD + row, 8), :] = live
        return carry

    lax.fori_loop(0, blocks, fill, 0)
    link = jnp.broadcast_to(link_ref[...], (8, link_ref.shape[1]))
    for k in range(2):
        for f in range(8):
            top = cells[f, k, pl.ds(PAD, 8), :]
            cells[f, k, pl.ds(0, 8), :] = jnp.take_along_axis(top, link, axis=1)
            below = cells[f, k, pl.ds(0, 1), :]
            cells[f, k, pl.ds(PAD - 1, 1), :] = below
            last = cells[f, k, pl.ds(PAD + nj - 1, 1), :]
            if f == LIVE:
                last = jnp.ones_like(last)
            cells[f, k, pl.ds(PAD + nj, 8), :] = jnp.broadcast_to(last, (8, last.shape[1]))

    def normal(b, carry):
        row = rows(b)
        for k in range(2):
            left = [cells[f, k, pl.ds(PAD - 1 + row, 8), :] for f in range(8)]
            right = [cells[f, k, pl.ds(PAD + row, 8), :] for f in range(8)]
            flux = roe(*walled(left, right, 1), 1, g1)
            for f in range(5):
                faces[f, k, pl.ds(row, 8), :] = flux[f]
        return carry

    lax.fori_loop(0, blocks + 1, normal, 0)

    def rest(b, carry):
        row = rows(b)
        near = [[cells[f, k, pl.ds(PAD + row, 8), :] for f in range(8)] for k in range(2)]
        halo = primitives(*[halo_ref[f, pl.ds(row, 8), :] for f in range(5)])
        inner = roe(near[0], near[1], 2, g2)
        edge = physical([jnp.where(first, near[0][f], near[1][f]) for f in range(7)], 2, g2)
        left = [jnp.where(first, near[1][f], halo[f]) for f in range(7)]
        right = [jnp.where(first, halo[f], near[0][f]) for f in range(7)]
        outer = roe(left, right, 2, g2)
        for k in range(2):
            here = near[k]
            lanes = here[0].shape[1]
            ahead = [pltpu.roll(x, lanes - 1, 1) for x in here]
            chord = roe(*walled(here, ahead, 0), 0, g0)
            for f in range(5):
                after = faces[f, k, pl.ds(row + 1, 8), :] - faces[f, k, pl.ds(row, 8), :]
                after = after + (chord[f] - pltpu.roll(chord[f], 1, 1))
                if k == 0:
                    span = inner[f] - jnp.where(first, edge[f], outer[f])
                else:
                    span = jnp.where(first, outer[f], edge[f]) - inner[f]
                emit(f, k, row, span + after)
        return carry

    lax.fori_loop(0, blocks, rest, 0)


def scratch(nj, ni):
    return [
        pltpu.VMEM((8, 2, nj + 2 * PAD, ni), jnp.float32),
        pltpu.VMEM((5, 2, nj + PAD, ni), jnp.float32),
    ]


def packed(f, row, q, nj):
    return pl.ds(4 * (f * nj + row) + q, 8, stride=4)


def first_kernel(place_ref, speed_ref, state_ref, halo_ref, mask_ref, link_ref, out_ref, cells, faces):
    nj = mask_ref.shape[1]

    def load(f, k, row):
        return state_ref[f, k, pl.ds(row, 8), :]

    def emit(f, k, row, div):
        out_ref[packed(f, row, k, nj), :] = load(f, k, row)
        out_ref[packed(f, row, 2 + k, nj), :] = div

    used = 4 * 5 * nj
    if out_ref.shape[0] > used:
        out_ref[used:, :] = jnp.zeros((out_ref.shape[0] - used, out_ref.shape[1]), jnp.float32)
    divergence_blocks(load, halo_ref, mask_ref, link_ref, speed_ref, place_ref[0], cells, faces, emit)


def last_kernel(place_ref, speed_ref, turned_ref, halo_ref, mask_ref, dtau_ref, link_ref, out_ref, cells, faces):
    nj = mask_ref.shape[1]

    def load(f, k, row):
        return turned_ref[packed(f, row, k, nj), :]

    def emit(f, k, row, div):
        old = load(f, k, row)
        residual = div + turned_ref[packed(f, row, 2 + k, nj), :]
        live = mask_ref[k, pl.ds(row, 8), :] > 0
        new = old - dtau_ref[k, pl.ds(row, 8), :] * residual
        out_ref[f, k, pl.ds(row, 8), :] = jnp.where(live, new, old)

    divergence_blocks(load, halo_ref, mask_ref, link_ref, speed_ref, place_ref[0], cells, faces, emit)


def edge_kernel(place_ref, turned_ref, out_ref):
    nj = out_ref.shape[1]
    for f in range(5):
        for row in range(0, nj, 8):
            out_ref[f, pl.ds(row, 8), :] = turned_ref[packed(f, row, place_ref[0], nj), :]


def instances_kernel(chunk_ref, matrix_ref, turned_ref, dtau_ref, mask_ref, out_ref):
    count = matrix_ref.shape[0]
    nj = mask_ref.shape[1]
    j = lax.rem(chunk_ref[0], nj)
    parts = [turned_ref[pl.ds(q, count, stride=4), :] for q in range(4)]
    state = jnp.concatenate(parts[:2], axis=1)
    div = jnp.concatenate(parts[2:], axis=1)
    dtau = jnp.concatenate([dtau_ref[k, pl.ds(j, 1), :] for k in range(2)], axis=1)
    mask = jnp.concatenate([mask_ref[k, pl.ds(j, 1), :] for k in range(2)], axis=1)
    matrix = matrix_ref[...]

    def times(x):
        return jnp.dot(matrix, x, precision=lax.Precision.HIGHEST, preferred_element_type=jnp.float32)

    new = state - dtau * (div + times(state))
    new = jnp.where(mask > 0, new, state)
    coupled = times(new)
    lanes = dtau_ref.shape[2]
    for q, value in enumerate((new[:, :lanes], new[:, lanes:], coupled[:, :lanes], coupled[:, lanes:])):
        out_ref[pl.ds(q, count, stride=4), :] = value


def call(kernel, shape, args, smem, scratch_shapes=(), flops=0):
    vmem = pl.BlockSpec(memory_space=pltpu.VMEM)
    specs = [pl.BlockSpec(memory_space=pltpu.SMEM)] * smem + [vmem] * (len(args) - smem)
    args = list(args[:smem]) + [pltpu.with_memory_space_constraint(a, pltpu.VMEM) for a in args[smem:]]
    return pl.pallas_call(
        kernel,
        out_shape=pltpu.VMEM(shape, jnp.float32),
        in_specs=specs,
        out_specs=vmem,
        scratch_shapes=list(scratch_shapes),
        cost_estimate=pl.CostEstimate(flops=flops, bytes_accessed=4 * math.prod(shape), transcendentals=0),
        compiler_params=pltpu.CompilerParams(vmem_limit_bytes=24 * 2**20),
    )(*args)


def shards(matrix, state, frame_velocity, dtau, live_mask, link):
    nj, ni = live_mask.shape[1:]
    flaps, gusts = lax.axis_size("flap"), lax.axis_size("gust")
    count = flaps * gusts
    field = state[0, 0]
    speed = frame_velocity[0, 0]
    link = link[None]
    span = lax.axis_index("span")
    first = jnp.where(span == 0, 1, 0).astype(jnp.int32)[None]
    chunk = (lax.axis_index("flap") * gusts + lax.axis_index("gust")).astype(jnp.int32)[None]
    swap = [(0, 1), (1, 0)]

    def turn(x):
        y = lax.all_to_all(x.reshape(count, 4, ni), ("flap", "gust"), 0, 0, tiled=True)
        return y.reshape(count * 4, ni)

    with jax.named_scope("halo"):
        halo = lax.ppermute(jnp.where(span == 0, field[:, 1], field[:, 0]), "span", swap)
    with jax.named_scope("first_divergence"):
        pack = call(
            first_kernel, (count * 4, ni), (first, speed, field, halo, live_mask, link), 2, scratch(nj, ni), 10**7
        )
    with jax.named_scope("turn"):
        pack = turn(pack)
    with jax.named_scope("instances"):
        pack = call(instances_kernel, (count * 4, ni), (chunk, matrix, pack, dtau, live_mask), 1, (), 10**8)
    with jax.named_scope("turn_back"):
        pack = turn(pack)
    with jax.named_scope("halo"):
        edge = call(edge_kernel, (5, nj, ni), (first, pack), 1)
        halo = lax.ppermute(edge, "span", swap)
    with jax.named_scope("last_divergence"):
        out = call(
            last_kernel,
            field.shape,
            (first, speed, pack, halo, live_mask, dtau, link),
            2,
            scratch(nj, ni),
            10**7,
        )
    return out[None, None]


def solution(mesh):
    flap = instance_matrix(mesh.shape["flap"], FLAP_OMEGA)
    gust = instance_matrix(mesh.shape["gust"], GUST_OMEGA)
    matrix = np.kron(flap, np.eye(len(gust))) + np.kron(np.eye(len(flap)), gust)
    matrix = jnp.asarray(matrix.astype(np.float32))
    in_specs = (
        P("flap", "gust", None, "span", None, None),
        P("flap", "gust", None),
        P("span", None, None),
        P("span", None, None),
        P(),
    )
    out_specs = P("flap", "gust", None, "span", None, None)
    return jax.shard_map(
        functools.partial(shards, matrix), mesh=mesh, in_specs=in_specs, out_specs=out_specs, check_vma=False
    )
```

time: 356 us -> 88.7 us (0.25)
  the two profiles are of different devices: /device:TPU:2 before, /device:TPU:1 now
where the time goes in v1:
time: 88.7 us; the launch traced here: 88.4 us
  starting transfers between devices  32 us (36%)
  blocking collectives  27.4 us (31%)
  waiting for transfers between devices  20.1 us (23%)
  Pallas kernels  6.43 us (7%)
  local copies, waits for them, and re-layouts  2.34 us (3%)
    all_to_all x1, blocking collectives, turn(): lax.all_to_all(x.reshape(count, 4, ni), ('flap', 'gust'), 0, 0, tiled=True)  27.4 us
    all_to_all x1, waiting for transfers between devices, turn(): lax.all_to_all(x.reshape(count, 4, ni), ('flap', 'gust'), 0, 0, tiled=True)  18.2 us
    all_to_all x1, starting transfers between devices, turn(): lax.all_to_all(x.reshape(count, 4, ni), ('flap', 'gust'), 0, 0, tiled=True)  17.1 us
    ppermute x1, starting transfers between devices, shards(): lax.ppermute(jnp.where(span == 0, field[:, 1], field[:, 0]), 'span', swap)  8.92 us
    pallas_call x4, Pallas kernels, call(): pl.pallas_call(kernel, out_shape=pltpu.VMEM(shape, jnp.float32), in_specs...  6.43 us
    ppermute x1, starting transfers between devices, shards(): halo = lax.ppermute(edge, 'span', swap)  5.94 us
    unnamed x14, local copies, waits for them, and re-layouts  2.34 us
  transfers between devices with their start and end apart: 3, of which 3 were waited for; matrix products, arithmetic and copies ran while one was open for 0% of the time, Pallas kernels for 0%

profile of v1, /device:TPU:1, one launch (start us, length us, event | category | flops | bytes accessed | tf_op | source)
XLA Modules:
  0.0 88.4 jit_solution(18370326441548329164)
XLA Ops:
  0.0 1.0 %copy.11 = f32[1,1,5,2,48,128]{5,4,2,3,1,0:T(8,128)S(1)} copy(f32[1,1,5,2,48,128]{5,4,3,2,1,0:T(8,128)} %param.6) | data formatting | bytes 491520 | tf_op args[0]
  1.0 0.0 copy-start
  1.0 0.0 copy-start.1
  1.0 8.9 %collective-permute-start = (f32[5,48,128]{2,1,0:T(8,128)S(1)}, f32[5,48,128]{2,1,0:T(8,128)S(1)}, u32[]{:S(2)}, u32[]{:S(2)}) collective-permute-start(f32[5,48,128]{2,1,0:T(8,128)S(1)} %fusion), channel_id=1, source_target_pairs={{0,1},{1,0},{2,3},{3,2},{4,5},{5,4},{6,7},{7,6},{8,9},{9,8},{10,11... | collective-permute-start | bytes 368648 | tf_op jit(solution)/shard_map/halo/ppermute | solution.py:283
  9.9 0.9 %collective-permute-done.halo_ref = f32[5,48,128]{2,1,0:T(8,128)S(1)} collective-permute-done((f32[5,48,128]{2,1,0:T(8,128)S(1)}, f32[5,48,128]{2,1,0:T(8,128)S(1)}, u32[]{:S(2)}, u32[]{:S(2)}) %collective-permute-start) | collective-permute-done | bytes 122912 | tf_op jit(solution)/shard_map/halo/ppermute | solution.py:283
  10.9 0.0 copy-start.4
  10.9 0.0 copy-start.5
  10.9 0.0 copy-done
  10.9 0.0 copy-done.1
  10.9 0.6 copy-done.4
  11.6 0.0 copy-done.5
  11.6 3.1 %first_divergence.1 = f32[1024,128]{1,0:T(8,128)} custom-call(s32[1]{0:T(128)} %bitcast.place_ref, f32[3]{0:T(128)S(1)} %bitcast.21, f32[5,2,48,128]{3,2,1,0:T(8,128)S(1)} %bitcast.20, f32[5,48,128]{2,1,0:T(8,128)S(1)} %collective-permute-done.halo_ref, s32[2,48,128]{2,1,0:T(8,128)S(1)} %copy-done.1, s32[1,128]{1,0:T(1,128)S(1)} %bitcast.23), custom_call_target="tpu_custom_call" | custom-call | flops 10000000 | bytes 524288 | tf_op jit(solution)/shard_map/first_divergence/pallas_call | solution.py:255
  14.6 0.0 copy-start.2
  14.6 0.0 copy-start.3
  14.6 17.1 %all-to-all-start = ((f32[256,4,128]{2,1,0:T(4,128)}), f32[256,4,128]{2,1,0:T(4,128)S(1)}, u32[]{:S(2)}, u32[]{:S(2)}) async-start(f32[256,4,128]{2,1,0:T(4,128)} %bitcast.7), calls=%async_computation | async-start | bytes 1048576 | tf_op jit(solution)/shard_map/turn/all_to_all | solution.py:279
  31.8 18.2 %all-to-all-done = f32[256,4,128]{2,1,0:T(4,128)S(1)} async-done(((f32[256,4,128]{2,1,0:T(4,128)}), f32[256,4,128]{2,1,0:T(4,128)S(1)}, u32[]{:S(2)}, u32[]{:S(2)}) %all-to-all-start) | async-done | bytes 524320 | tf_op jit(solution)/shard_map/turn/all_to_all | solution.py:279
  50.0 0.0 copy-done.2
  50.0 0.0 copy-done.3
  50.0 1.1 %instances.1 = f32[1024,128]{1,0:T(8,128)S(1)} custom-call(s32[1]{0:T(128)} %bitcast.2.chunk_ref, f32[256,256]{1,0:T(8,128)S(1)} %copy-done.2, f32[1024,128]{1,0:T(8,128)S(1)} %bitcast.18, f32[2,48,128]{2,1,0:T(8,128)S(1)} %copy-done.3, s32[2,48,128]{2,1,0:T(8,128)S(1)} %copy-done.1), custom_call_target="tpu_custom_call" | custom-call | flops 100000000 | bytes 524288 | tf_op jit(solution)/shard_map/instances/pallas_call | solution.py:255
  51.1 27.4 %all_to_all.10 = f32[256,4,128]{2,1,0:T(4,128)S(1)} all-to-all(f32[256,4,128]{2,1,0:T(4,128)S(1)} %bitcast.19), channel_id=1, replica_groups=mesh['flap'=16,'gust'=16,'span'=2] {'flap','gust'}, dimensions={0} | all-to-all | bytes 1048576 | tf_op jit(solution)/shard_map/turn_back/all_to_all | solution.py:279
  78.5 5.9 %collective-permute-start.1 = (f32[5,48,128]{2,1,0:T(8,128)S(1)}, f32[5,48,128]{2,1,0:T(8,128)S(1)}, u32[]{:S(2)}, u32[]{:S(2)}) collective-permute-start(f32[5,48,128]{2,1,0:T(8,128)S(1)} %halo.1), channel_id=1, source_target_pairs={{0,1},{1,0},{2,3},{3,2},{4,5},{5,4},{6,7},{7,6},{8,9},{9,8},{10,11... | collective-permute-start | bytes 368648 | tf_op jit(solution)/shard_map/halo/ppermute | solution.py:296
  84.4 1.0 %collective-permute-done.1.halo_ref = f32[5,48,128]{2,1,0:T(8,128)S(1)} collective-permute-done((f32[5,48,128]{2,1,0:T(8,128)S(1)}, f32[5,48,128]{2,1,0:T(8,128)S(1)}, u32[]{:S(2)}, u32[]{:S(2)}) %collective-permute-start.1) | collective-permute-done | bytes 122912 | tf_op jit(solution)/shard_map/halo/ppermute | solution.py:296
  85.4 2.3 %last_divergence.1 = f32[5,2,48,128]{3,2,1,0:T(8,128)S(1)} custom-call(s32[1]{0:T(128)} %bitcast.place_ref, f32[3]{0:T(128)S(1)} %bitcast.22, f32[1024,128]{1,0:T(8,128)S(1)} %bitcast.17, f32[5,48,128]{2,1,0:T(8,128)S(1)} %collective-permute-done.1.halo_ref, s32[2,48,128]{2,1,0:T(8,128)S(1)} %copy-done.1, f32[2,48,128]{2,1,0:T(8,128)S(1)} %copy-done.3, ...), custom_call_target="tpu_custom_call" | custom-call | flops 10000000 | bytes 245760 | tf_op jit(solution)/shard_map/last_divergence/pallas_call | solution.py:255
  87.7 0.7 copy.12
  (2 shorter events, 0.0 us)
Async XLA Ops:
  1.0 9.9 %copy-start = (f32[1,1,5,2,48,128]{5,4,3,2,1,0:T(8,128)S(1)}, f32[1,1,5,2,48,128]{5,4,3,2,1,0:T(8,128)}, u32[]{:S(2)}) copy-start(f32[1,1,5,2,48,128]{5,4,3,2,1,0:T(8,128)} %param.6) | copy-start | bytes 737284
  1.0 9.9 %copy-start.1 = (s32[2,48,128]{2,1,0:T(8,128)S(1)}, s32[2,48,128]{2,1,0:T(8,128)}, u32[]{:S(2)}) copy-start(s32[2,48,128]{2,1,0:T(8,128)} %mask_ref.5) | copy-start | bytes 147460
  1.0 9.9 %collective-permute-start = (f32[5,48,128]{2,1,0:T(8,128)S(1)}, f32[5,48,128]{2,1,0:T(8,128)S(1)}, u32[]{:S(2)}, u32[]{:S(2)}) collective-permute-start(f32[5,48,128]{2,1,0:T(8,128)S(1)} %fusion), channel_id=1, source_target_pairs={{0,1},{1,0},{2,3},{3,2},{4,5},{5,4},{6,7},{7,6},{8,9},{9,8},{10,11... | collective-permute-start | bytes 368648 | tf_op jit(solution)/shard_map/halo/ppermute | solution.py:283
  10.9 0.7 copy-start.4
  10.9 0.7 copy-start.5
  14.6 35.3 %copy-start.2 = (f32[256,256]{1,0:T(8,128)S(1)}, f32[256,256]{1,0:T(8,128)}, u32[]{:S(2)}) copy-start(f32[256,256]{1,0:T(8,128)} %constant.20.clone.matrix_ref) | copy-start | bytes 786436
  14.6 35.3 %copy-start.3 = (f32[2,48,128]{2,1,0:T(8,128)S(1)}, f32[2,48,128]{2,1,0:T(8,128)}, u32[]{:S(2)}) copy-start(f32[2,48,128]{2,1,0:T(8,128)} %dtau_ref.3) | copy-start | bytes 147460
  14.6 35.3 %all-to-all-start = ((f32[256,4,128]{2,1,0:T(4,128)}), f32[256,4,128]{2,1,0:T(4,128)S(1)}, u32[]{:S(2)}, u32[]{:S(2)}) async-start(f32[256,4,128]{2,1,0:T(4,128)} %bitcast.7), calls=%async_computation | async-start | bytes 1048576 | tf_op jit(solution)/shard_map/turn/all_to_all | solution.py:279
  78.5 6.9 %collective-permute-start.1 = (f32[5,48,128]{2,1,0:T(8,128)S(1)}, f32[5,48,128]{2,1,0:T(8,128)S(1)}, u32[]{:S(2)}, u32[]{:S(2)}) collective-permute-start(f32[5,48,128]{2,1,0:T(8,128)S(1)} %halo.1), channel_id=1, source_target_pairs={{0,1},{1,0},{2,3},{3,2},{4,5},{5,4},{6,7},{7,6},{8,9},{9,8},{10,11... | collective-permute-start | bytes 368648 | tf_op jit(solution)/shard_map/halo/ppermute | solution.py:296

commit v2 on v1

--- a/solution.py
+++ b/solution.py
@@ -105,11 +105,10 @@
     return new_l, new_r
 
 
-def divergence_blocks(load, halo_ref, mask_ref, link_ref, speed_ref, first, cells, faces, emit):
+def most_of_divergence(load, mask_ref, link_ref, speed_ref, first, cells, faces, emit):
     nj = mask_ref.shape[1]
     blocks = nj // 8
     g0, g1, g2 = speed_ref[0], speed_ref[1], speed_ref[2]
-    first = first > 0
 
     def rows(b):
         return pl.multiple_of(8 * b, 8)
@@ -129,8 +128,7 @@
     for k in range(2):
         for f in range(8):
             top = cells[f, k, pl.ds(PAD, 8), :]
-            cells[f, k, pl.ds(0, 8), :] = jnp.take_along_axis(top, link, axis=1)
-            below = cells[f, k, pl.ds(0, 1), :]
+            below = jnp.take_along_axis(top, link, axis=1)[:1]
             cells[f, k, pl.ds(PAD - 1, 1), :] = below
             last = cells[f, k, pl.ds(PAD + nj - 1, 1), :]
             if f == LIVE:
@@ -152,12 +150,8 @@
     def rest(b, carry):
         row = rows(b)
         near = [[cells[f, k, pl.ds(PAD + row, 8), :] for f in range(8)] for k in range(2)]
-        halo = primitives(*[halo_ref[f, pl.ds(row, 8), :] for f in range(5)])
         inner = roe(near[0], near[1], 2, g2)
         edge = physical([jnp.where(first, near[0][f], near[1][f]) for f in range(7)], 2, g2)
-        left = [jnp.where(first, near[1][f], halo[f]) for f in range(7)]
-        right = [jnp.where(first, halo[f], near[0][f]) for f in range(7)]
-        outer = roe(left, right, 2, g2)
         for k in range(2):
             here = near[k]
             lanes = here[0].shape[1]
@@ -167,13 +161,21 @@
                 after = faces[f, k, pl.ds(row + 1, 8), :] - faces[f, k, pl.ds(row, 8), :]
                 after = after + (chord[f] - pltpu.roll(chord[f], 1, 1))
                 if k == 0:
-                    span = inner[f] - jnp.where(first, edge[f], outer[f])
+                    span = inner[f] - jnp.where(first, edge[f], 0.0)
                 else:
-                    span = jnp.where(first, outer[f], edge[f]) - inner[f]
+                    span = jnp.where(first, 0.0, edge[f]) - inner[f]
                 emit(f, k, row, span + after)
         return carry
 
     lax.fori_loop(0, blocks, rest, 0)
+
+
+def outer_face(mine, other, speed_ref, first):
+    mine, other = primitives(*mine), primitives(*other)
+    left = [jnp.where(first, a, b) for a, b in zip(mine, other)]
+    right = [jnp.where(first, b, a) for a, b in zip(mine, other)]
+    sign = jnp.where(first, 1.0, -1.0)
+    return [sign * x for x in roe(left, right, 2, speed_ref[2])]
 
 
 def scratch(nj, ni):
@@ -187,36 +189,65 @@
     return pl.ds(4 * (f * nj + row) + q, 8, stride=4)
 
 
-def first_kernel(place_ref, speed_ref, state_ref, halo_ref, mask_ref, link_ref, out_ref, cells, faces):
-    nj = mask_ref.shape[1]
-
+def first_kernel(place_ref, speed_ref, state_ref, mask_ref, link_ref, out_ref, cells, faces):
     def load(f, k, row):
         return state_ref[f, k, pl.ds(row, 8), :]
 
     def emit(f, k, row, div):
-        out_ref[packed(f, row, k, nj), :] = load(f, k, row)
-        out_ref[packed(f, row, 2 + k, nj), :] = div
-
+        out_ref[f, k, pl.ds(row, 8), :] = div
+
+    most_of_divergence(load, mask_ref, link_ref, speed_ref, place_ref[0] > 0, cells, faces, emit)
+
+
+def first_edge_kernel(place_ref, speed_ref, state_ref, other_ref, div_ref, out_ref):
+    nj = state_ref.shape[2]
+    edge = place_ref[0]
+    first = edge > 0
     used = 4 * 5 * nj
     if out_ref.shape[0] > used:
         out_ref[used:, :] = jnp.zeros((out_ref.shape[0] - used, out_ref.shape[1]), jnp.float32)
-    divergence_blocks(load, halo_ref, mask_ref, link_ref, speed_ref, place_ref[0], cells, faces, emit)
-
-
-def last_kernel(place_ref, speed_ref, turned_ref, halo_ref, mask_ref, dtau_ref, link_ref, out_ref, cells, faces):
+    for row in range(0, nj, 8):
+        block = pl.ds(row, 8)
+        mine = [state_ref[f, edge, block, :] for f in range(5)]
+        other = [other_ref[f, 1 - edge, block, :] for f in range(5)]
+        flux = outer_face(mine, other, speed_ref, first)
+        for f in range(5):
+            out_ref[packed(f, row, edge, nj), :] = mine[f]
+            out_ref[packed(f, row, 1 - edge, nj), :] = state_ref[f, 1 - edge, block, :]
+            out_ref[packed(f, row, 2 + edge, nj), :] = div_ref[f, edge, block, :] + flux[f]
+            out_ref[packed(f, row, 3 - edge, nj), :] = div_ref[f, 1 - edge, block, :]
+
+
+def last_kernel(place_ref, speed_ref, turned_ref, mask_ref, link_ref, out_ref, cells, faces):
     nj = mask_ref.shape[1]
 
     def load(f, k, row):
         return turned_ref[packed(f, row, k, nj), :]
 
     def emit(f, k, row, div):
-        old = load(f, k, row)
-        residual = div + turned_ref[packed(f, row, 2 + k, nj), :]
-        live = mask_ref[k, pl.ds(row, 8), :] > 0
-        new = old - dtau_ref[k, pl.ds(row, 8), :] * residual
-        out_ref[f, k, pl.ds(row, 8), :] = jnp.where(live, new, old)
-
-    divergence_blocks(load, halo_ref, mask_ref, link_ref, speed_ref, place_ref[0], cells, faces, emit)
+        out_ref[f, k, pl.ds(row, 8), :] = div + turned_ref[packed(f, row, 2 + k, nj), :]
+
+    most_of_divergence(load, mask_ref, link_ref, speed_ref, place_ref[0] > 0, cells, faces, emit)
+
+
+def last_edge_kernel(place_ref, speed_ref, turned_ref, other_ref, residual_ref, mask_ref, dtau_ref, out_ref):
+    nj = mask_ref.shape[1]
+    edge = place_ref[0]
+    first = edge > 0
+    for row in range(0, nj, 8):
+        block = pl.ds(row, 8)
+        mine = [turned_ref[packed(f, row, edge, nj), :] for f in range(5)]
+        flux = outer_face(mine, [other_ref[f, block, :] for f in range(5)], speed_ref, first)
+        for k in (edge, 1 - edge):
+            live = mask_ref[k, block, :] > 0
+            dtau = dtau_ref[k, block, :]
+            for f in range(5):
+                residual = residual_ref[f, k, block, :]
+                if k is edge:
+                    old, residual = mine[f], residual + flux[f]
+                else:
+                    old = turned_ref[packed(f, row, k, nj), :]
+                out_ref[f, k, block, :] = jnp.where(live, old - dtau * residual, old)
 
 
 def edge_kernel(place_ref, turned_ref, out_ref):
@@ -248,13 +279,13 @@
         out_ref[pl.ds(q, count, stride=4), :] = value
 
 
-def call(kernel, shape, args, smem, scratch_shapes=(), flops=0):
+def call(kernel, shape, args, smem, scratch_shapes=(), flops=0, keep=True):
     vmem = pl.BlockSpec(memory_space=pltpu.VMEM)
     specs = [pl.BlockSpec(memory_space=pltpu.SMEM)] * smem + [vmem] * (len(args) - smem)
     args = list(args[:smem]) + [pltpu.with_memory_space_constraint(a, pltpu.VMEM) for a in args[smem:]]
     return pl.pallas_call(
         kernel,
-        out_shape=pltpu.VMEM(shape, jnp.float32),
+        out_shape=pltpu.VMEM(shape, jnp.float32) if keep else jax.ShapeDtypeStruct(shape, jnp.float32),
         in_specs=specs,
         out_specs=vmem,
         scratch_shapes=list(scratch_shapes),
@@ -270,8 +301,7 @@
     field = state[0, 0]
     speed = frame_velocity[0, 0]
     link = link[None]
-    span = lax.axis_index("span")
-    first = jnp.where(span == 0, 1, 0).astype(jnp.int32)[None]
+    first = jnp.where(lax.axis_index("span") == 0, 1, 0).astype(jnp.int32)[None]
     chunk = (lax.axis_index("flap") * gusts + lax.axis_index("gust")).astype(jnp.int32)[None]
     swap = [(0, 1), (1, 0)]
 
@@ -280,11 +310,10 @@
         return y.reshape(count * 4, ni)
 
     with jax.named_scope("halo"):
-        halo = lax.ppermute(jnp.where(span == 0, field[:, 1], field[:, 0]), "span", swap)
+        other = lax.ppermute(field, "span", swap)
     with jax.named_scope("first_divergence"):
-        pack = call(
-            first_kernel, (count * 4, ni), (first, speed, field, halo, live_mask, link), 2, scratch(nj, ni), 10**7
-        )
+        div = call(first_kernel, field.shape, (first, speed, field, live_mask, link), 2, scratch(nj, ni), 10**8)
+        pack = call(first_edge_kernel, (count * 4, ni), (first, speed, field, other, div), 2)
     with jax.named_scope("turn"):
         pack = turn(pack)
     with jax.named_scope("instances"):
@@ -292,16 +321,11 @@
     with jax.named_scope("turn_back"):
         pack = turn(pack)
     with jax.named_scope("halo"):
-        edge = call(edge_kernel, (5, nj, ni), (first, pack), 1)
-        halo = lax.ppermute(edge, "span", swap)
+        other = lax.ppermute(call(edge_kernel, (5, nj, ni), (first, pack), 1), "span", swap)
     with jax.named_scope("last_divergence"):
+        residual = call(last_kernel, field.shape, (first, speed, pack, live_mask, link), 2, scratch(nj, ni), 10**8)
         out = call(
-            last_kernel,
-            field.shape,
-            (first, speed, pack, halo, live_mask, dtau, link),
-            2,
-            scratch(nj, ni),
-            10**7,
+            last_edge_kernel, field.shape, (first, speed, pack, other, residual, live_mask, dtau), 2, keep=False
         )
     return out[None, None]
 

time: 88.7 us -> 89.3 us (level)
  Pallas kernels: 6.43 us -> 8.59 us
  waiting for transfers between devices: 20.1 us -> 18.9 us
    pallas_call x4 -> x6, Pallas kernels: 6.43 us -> 8.59 us  [call(): pl.pallas_call(kernel, out_shape=pltpu.VMEM(shape, jnp.float32) if keep e...]
    ppermute x2, waiting for transfers between devices: 1.9 us -> 0.01 us  [the longest x1 0.01 us: shards(): lax.ppermute(call(edge_kernel, (5, nj, ni), (first, pack), 1), 'span', swap)]
  transfers between devices with their start and end apart: 3 -> 3, of which waited for: 3 -> 1; matrix products, arithmetic and copies ran while one was open for 0% -> 0% of each run, Pallas kernels for 0% -> 5%
where the time goes in v2:
time: 89.3 us; the launch traced here: 89 us
  starting transfers between devices  31.5 us (35%)
  blocking collectives  27.5 us (31%)
  waiting for transfers between devices  18.9 us (21%)
  Pallas kernels  8.59 us (10%)
  local copies, waits for them, and re-layouts  2.41 us (3%)
    all_to_all x1, blocking collectives, turn(): lax.all_to_all(x.reshape(count, 4, ni), ('flap', 'gust'), 0, 0, tiled=True)  27.5 us
    all_to_all x1, waiting for transfers between devices, turn(): lax.all_to_all(x.reshape(count, 4, ni), ('flap', 'gust'), 0, 0, tiled=True)  18.9 us
    all_to_all x1, starting transfers between devices, turn(): lax.all_to_all(x.reshape(count, 4, ni), ('flap', 'gust'), 0, 0, tiled=True)  17.1 us
    ppermute x1, starting transfers between devices, shards(): other = lax.ppermute(field, 'span', swap)  8.77 us
    pallas_call x6, Pallas kernels, call(): pl.pallas_call(kernel, out_shape=pltpu.VMEM(shape, jnp.float32) if keep e...  8.59 us
    ppermute x1, starting transfers between devices, shards(): lax.ppermute(call(edge_kernel, (5, nj, ni), (first, pack), 1), 'span', swap)  5.56 us
    unnamed x14, local copies, waits for them, and re-layouts  2.41 us
  transfers between devices with their start and end apart: 3, of which 1 were waited for; matrix products, arithmetic and copies ran while one was open for 0% of the time, Pallas kernels for 5%

profile of v2, /device:TPU:1, one launch (start us, length us, event | category | flops | bytes accessed | tf_op | source)
XLA Modules:
  0.0 89.0 jit_solution(6346353953159718862)
XLA Ops:
  0.0 8.8 %collective-permute-start = (f32[5,2,48,128]{3,2,1,0:T(8,128)}, f32[5,2,48,128]{3,2,1,0:T(8,128)S(1)}, u32[]{:S(2)}, u32[]{:S(2)}) collective-permute-start(f32[5,2,48,128]{3,2,1,0:T(8,128)} %bitcast.15), channel_id=1, source_target_pairs={{0,1},{1,0},{2,3},{3,2},{4,5},{5,4},{6,7},{7,6},{8,9},{9,8},{10,11... | collective-permute-start | bytes 737288 | tf_op jit(solution)/shard_map/halo/ppermute | solution.py:313
  8.8 0.0 copy-start.5
  8.8 0.0 copy-start.6
  8.8 0.6 copy-done.5
  9.4 0.0 copy-done.6
  9.5 0.0 copy-start
  9.5 0.9 %copy-done = f32[1,1,5,2,48,128]{5,4,3,2,1,0:T(8,128)S(1)} copy-done((f32[1,1,5,2,48,128]{5,4,3,2,1,0:T(8,128)S(1)}, f32[1,1,5,2,48,128]{5,4,3,2,1,0:T(8,128)}, u32[]{:S(2)}) %copy-start) | copy-done | bytes 245784
  10.4 0.8 copy-done.1
  11.2 2.2 %first_divergence.2.div_ref = f32[5,2,48,128]{3,2,1,0:T(8,128)S(1)} custom-call(s32[1]{0:T(128)} %bitcast.place_ref, f32[3]{0:T(128)S(1)} %bitcast.18, f32[5,2,48,128]{3,2,1,0:T(8,128)S(1)} %bitcast.16, s32[2,48,128]{2,1,0:T(8,128)S(1)} %copy-done.1, s32[1,128]{1,0:T(1,128)S(1)} %bitcast.22), custom_call_target="tpu_custom_call" | custom-call | flops 100000000 | bytes 245760 | tf_op jit(solution)/shard_map/first_divergence/pallas_call | solution.py:286
  13.5 0.0 collective-permute-done.other_ref
  13.5 1.5 %first_divergence.3 = f32[1024,128]{1,0:T(8,128)} custom-call(s32[1]{0:T(128)} %bitcast.place_ref, f32[3]{0:T(128)S(1)} %bitcast.19, f32[5,2,48,128]{3,2,1,0:T(8,128)S(1)} %bitcast.17, f32[5,2,48,128]{3,2,1,0:T(8,128)S(1)} %collective-permute-done.other_ref, f32[5,2,48,128]{3,2,1,0:T(8,128)S(1)} %first_divergence.2.div_ref), custom_call_target="tpu_custom_call" | custom-call | bytes 524288 | tf_op jit(solution)/shard_map/first_divergence/pallas_call | solution.py:286
  15.0 0.0 copy-start.2
  15.0 0.0 copy-start.3
  15.0 17.1 %all-to-all-start = ((f32[256,4,128]{2,1,0:T(4,128)}), f32[256,4,128]{2,1,0:T(4,128)S(1)}, u32[]{:S(2)}, u32[]{:S(2)}) async-start(f32[256,4,128]{2,1,0:T(4,128)} %bitcast.5), calls=%async_computation | async-start | bytes 1048576 | tf_op jit(solution)/shard_map/turn/all_to_all | solution.py:309
  32.2 18.9 %all-to-all-done = f32[256,4,128]{2,1,0:T(4,128)S(1)} async-done(((f32[256,4,128]{2,1,0:T(4,128)}), f32[256,4,128]{2,1,0:T(4,128)S(1)}, u32[]{:S(2)}, u32[]{:S(2)}) %all-to-all-start) | async-done | bytes 524320 | tf_op jit(solution)/shard_map/turn/all_to_all | solution.py:309
  51.0 0.0 copy-done.2
  51.0 0.0 copy-done.3
  51.0 0.0 copy-done.4
  51.0 1.1 %instances.1 = f32[1024,128]{1,0:T(8,128)S(1)} custom-call(s32[1]{0:T(128)} %bitcast.2.chunk_ref, f32[256,256]{1,0:T(8,128)S(1)} %copy-done.3, f32[1024,128]{1,0:T(8,128)S(1)} %bitcast.13, f32[2,48,128]{2,1,0:T(8,128)S(1)} %copy-done.4, s32[2,48,128]{2,1,0:T(8,128)S(1)} %copy-done.2), custom_call_target="tpu_custom_call" | custom-call | flops 100000000 | bytes 524288 | tf_op jit(solution)/shard_map/instances/pallas_call | solution.py:286
  52.1 27.5 %all_to_all.10 = f32[256,4,128]{2,1,0:T(4,128)S(1)} all-to-all(f32[256,4,128]{2,1,0:T(4,128)S(1)} %bitcast.14), channel_id=1, replica_groups=mesh['flap'=16,'gust'=16,'span'=2] {'flap','gust'}, dimensions={0} | all-to-all | bytes 1048576 | tf_op jit(solution)/shard_map/turn_back/all_to_all | solution.py:309
  79.7 5.6 %collective-permute-start.1 = (f32[5,48,128]{2,1,0:T(8,128)S(1)}, f32[5,48,128]{2,1,0:T(8,128)S(1)}, u32[]{:S(2)}, u32[]{:S(2)}) collective-permute-start(f32[5,48,128]{2,1,0:T(8,128)S(1)} %halo.1), channel_id=1, source_target_pairs={{0,1},{1,0},{2,3},{3,2},{4,5},{5,4},{6,7},{7,6},{8,9},{9,8},{10,11... | collective-permute-start | bytes 368648 | tf_op jit(solution)/shard_map/halo/ppermute | solution.py:324
  85.2 2.3 %last_divergence.2.residual_ref = f32[5,2,48,128]{3,2,1,0:T(8,128)S(1)} custom-call(s32[1]{0:T(128)} %bitcast.place_ref, f32[3]{0:T(128)S(1)} %bitcast.20, f32[1024,128]{1,0:T(8,128)S(1)} %bitcast.11, s32[2,48,128]{2,1,0:T(8,128)S(1)} %copy-done.2, s32[1,128]{1,0:T(1,128)S(1)} %bitcast.23), custom_call_target="tpu_custom_call" | custom-call | flops 100000000 | bytes 245760 | tf_op jit(solution)/shard_map/last_divergence/pallas_call | solution.py:286
  87.5 0.0 collective-permute-done.1.other_ref
  87.5 1.5 %last_divergence.3 = f32[5,2,48,128]{3,2,1,0:T(8,128)} custom-call(s32[1]{0:T(128)} %bitcast.place_ref, f32[3]{0:T(128)S(1)} %bitcast.21, f32[1024,128]{1,0:T(8,128)S(1)} %bitcast.12, f32[5,48,128]{2,1,0:T(8,128)S(1)} %collective-permute-done.1.other_ref, f32[5,2,48,128]{3,2,1,0:T(8,128)S(1)} %last_divergence.2.residual_ref, s32[2,48,128]{2,1,0:T(8,128)S(1)} %copy-done.2, ...), custom_call_target="tpu_custom_call" | custom-call | bytes 245760 | tf_op jit(solution)/shard_map/last_divergence/pallas_call | solution.py:286
  (3 shorter events, 0.0 us)
Async XLA Ops:
  0.0 13.5 %collective-permute-start = (f32[5,2,48,128]{3,2,1,0:T(8,128)}, f32[5,2,48,128]{3,2,1,0:T(8,128)S(1)}, u32[]{:S(2)}, u32[]{:S(2)}) collective-permute-start(f32[5,2,48,128]{3,2,1,0:T(8,128)} %bitcast.15), channel_id=1, source_target_pairs={{0,1},{1,0},{2,3},{3,2},{4,5},{5,4},{6,7},{7,6},{8,9},{9,8},{10,11... | collective-permute-start | bytes 737288 | tf_op jit(solution)/shard_map/halo/ppermute | solution.py:313
  8.8 0.7 copy-start.5
  8.8 0.7 copy-start.6
  9.5 0.9 %copy-start = (f32[1,1,5,2,48,128]{5,4,3,2,1,0:T(8,128)S(1)}, f32[1,1,5,2,48,128]{5,4,3,2,1,0:T(8,128)}, u32[]{:S(2)}) copy-start(f32[1,1,5,2,48,128]{5,4,3,2,1,0:T(8,128)} %param.6) | copy-start | bytes 737284
  10.4 0.8 copy-start.1
  15.0 36.0 %copy-start.2 = (s32[2,48,128]{2,1,0:T(8,128)S(1)}, s32[2,48,128]{2,1,0:T(8,128)}, u32[]{:S(2)}) copy-start(s32[2,48,128]{2,1,0:T(8,128)} %mask_ref.7) | copy-start | bytes 147460
  15.0 36.0 %copy-start.3 = (f32[256,256]{1,0:T(8,128)S(1)}, f32[256,256]{1,0:T(8,128)}, u32[]{:S(2)}) copy-start(f32[256,256]{1,0:T(8,128)} %constant.20.clone.matrix_ref) | copy-start | bytes 786436
  15.0 36.0 %copy-start.4 = (f32[2,48,128]{2,1,0:T(8,128)S(1)}, f32[2,48,128]{2,1,0:T(8,128)}, u32[]{:S(2)}) copy-start(f32[2,48,128]{2,1,0:T(8,128)} %dtau_ref.3) | copy-start | bytes 147460
  15.0 36.0 %all-to-all-start = ((f32[256,4,128]{2,1,0:T(4,128)}), f32[256,4,128]{2,1,0:T(4,128)S(1)}, u32[]{:S(2)}, u32[]{:S(2)}) async-start(f32[256,4,128]{2,1,0:T(4,128)} %bitcast.5), calls=%async_computation | async-start | bytes 1048576 | tf_op jit(solution)/shard_map/turn/all_to_all | solution.py:309
  79.7 7.8 %collective-permute-start.1 = (f32[5,48,128]{2,1,0:T(8,128)S(1)}, f32[5,48,128]{2,1,0:T(8,128)S(1)}, u32[]{:S(2)}, u32[]{:S(2)}) collective-permute-start(f32[5,48,128]{2,1,0:T(8,128)S(1)} %halo.1), channel_id=1, source_target_pairs={{0,1},{1,0},{2,3},{3,2},{4,5},{5,4},{6,7},{7,6},{8,9},{9,8},{10,11... | collective-permute-start | bytes 368648 | tf_op jit(solution)/shard_map/halo/ppermute | solution.py:324

commit v3 on v2

--- a/solution.py
+++ b/solution.py
@@ -105,10 +105,14 @@
     return new_l, new_r
 
 
+def frame(speed_ref, axis):
+    return jnp.broadcast_to(speed_ref[:, axis : axis + 1], (8, 128))
+
+
 def most_of_divergence(load, mask_ref, link_ref, speed_ref, first, cells, faces, emit):
     nj = mask_ref.shape[1]
     blocks = nj // 8
-    g0, g1, g2 = speed_ref[0], speed_ref[1], speed_ref[2]
+    g0, g1, g2 = [frame(speed_ref, axis) for axis in range(3)]
 
     def rows(b):
         return pl.multiple_of(8 * b, 8)
@@ -175,7 +179,7 @@
     left = [jnp.where(first, a, b) for a, b in zip(mine, other)]
     right = [jnp.where(first, b, a) for a, b in zip(mine, other)]
     sign = jnp.where(first, 1.0, -1.0)
-    return [sign * x for x in roe(left, right, 2, speed_ref[2])]
+    return [sign * x for x in roe(left, right, 2, frame(speed_ref, 2))]
 
 
 def scratch(nj, ni):
@@ -189,33 +193,45 @@
     return pl.ds(4 * (f * nj + row) + q, 8, stride=4)
 
 
-def first_kernel(place_ref, speed_ref, state_ref, mask_ref, link_ref, out_ref, cells, faces):
-    def load(f, k, row):
-        return state_ref[f, k, pl.ds(row, 8), :]
-
-    def emit(f, k, row, div):
-        out_ref[f, k, pl.ds(row, 8), :] = div
-
-    most_of_divergence(load, mask_ref, link_ref, speed_ref, place_ref[0] > 0, cells, faces, emit)
-
-
-def first_edge_kernel(place_ref, speed_ref, state_ref, other_ref, div_ref, out_ref):
-    nj = state_ref.shape[2]
-    edge = place_ref[0]
-    first = edge > 0
+def first_kernel(place_ref, *refs):
+    sources, targets, (out_ref, cells, faces, state_ref, sems) = refs[:6], refs[6:11], refs[11:]
+    mask_ref, link_ref, speed_ref = targets[:3]
+    nj = mask_ref.shape[1]
+    copies = [
+        pltpu.make_async_copy(source, target, sems.at[i])
+        for i, (source, target) in enumerate(zip(sources, (state_ref, *targets)))
+    ]
+    for copy in copies:
+        copy.start()
     used = 4 * 5 * nj
     if out_ref.shape[0] > used:
         out_ref[used:, :] = jnp.zeros((out_ref.shape[0] - used, out_ref.shape[1]), jnp.float32)
+    for copy in copies[:4]:
+        copy.wait()
+
+    def load(f, k, row):
+        return state_ref[f, k, pl.ds(row, 8), :]
+
+    def emit(f, k, row, div):
+        out_ref[packed(f, row, k, nj), :] = load(f, k, row)
+        out_ref[packed(f, row, 2 + k, nj), :] = div
+
+    most_of_divergence(load, mask_ref, link_ref, speed_ref, place_ref[0] > 0, cells, faces, emit)
+    for copy in copies[4:]:
+        copy.wait()
+
+
+def first_edge_kernel(place_ref, speed_ref, other_ref, pack_ref, out_ref):
+    nj = other_ref.shape[2]
+    edge = place_ref[0]
+    out_ref[...] = pack_ref[...]
     for row in range(0, nj, 8):
-        block = pl.ds(row, 8)
-        mine = [state_ref[f, edge, block, :] for f in range(5)]
-        other = [other_ref[f, 1 - edge, block, :] for f in range(5)]
-        flux = outer_face(mine, other, speed_ref, first)
+        mine = [pack_ref[packed(f, row, edge, nj), :] for f in range(5)]
+        other = [other_ref[f, 1 - edge, pl.ds(row, 8), :] for f in range(5)]
+        flux = outer_face(mine, other, speed_ref, edge > 0)
         for f in range(5):
-            out_ref[packed(f, row, edge, nj), :] = mine[f]
-            out_ref[packed(f, row, 1 - edge, nj), :] = state_ref[f, 1 - edge, block, :]
-            out_ref[packed(f, row, 2 + edge, nj), :] = div_ref[f, edge, block, :] + flux[f]
-            out_ref[packed(f, row, 3 - edge, nj), :] = div_ref[f, 1 - edge, block, :]
+            div = packed(f, row, 2 + edge, nj)
+            out_ref[div, :] = pack_ref[div, :] + flux[f]
 
 
 def last_kernel(place_ref, speed_ref, turned_ref, mask_ref, link_ref, out_ref, cells, faces):
@@ -257,10 +273,10 @@
             out_ref[f, pl.ds(row, 8), :] = turned_ref[packed(f, row, place_ref[0], nj), :]
 
 
-def instances_kernel(chunk_ref, matrix_ref, turned_ref, dtau_ref, mask_ref, out_ref):
+def instances_kernel(place_ref, matrix_ref, turned_ref, dtau_ref, mask_ref, out_ref):
     count = matrix_ref.shape[0]
     nj = mask_ref.shape[1]
-    j = lax.rem(chunk_ref[0], nj)
+    j = lax.rem(place_ref[1], nj)
     parts = [turned_ref[pl.ds(q, count, stride=4), :] for q in range(4)]
     state = jnp.concatenate(parts[:2], axis=1)
     div = jnp.concatenate(parts[2:], axis=1)
@@ -279,19 +295,40 @@
         out_ref[pl.ds(q, count, stride=4), :] = value
 
 
-def call(kernel, shape, args, smem, scratch_shapes=(), flops=0, keep=True):
+def call(kernel, shape, args, scratch_shapes=(), flops=0, aliases=None, keep=True):
     vmem = pl.BlockSpec(memory_space=pltpu.VMEM)
-    specs = [pl.BlockSpec(memory_space=pltpu.SMEM)] * smem + [vmem] * (len(args) - smem)
-    args = list(args[:smem]) + [pltpu.with_memory_space_constraint(a, pltpu.VMEM) for a in args[smem:]]
+    specs = [pl.BlockSpec(memory_space=pltpu.SMEM)] + [vmem] * (len(args) - 1)
+    args = [args[0]] + [pltpu.with_memory_space_constraint(a, pltpu.VMEM) for a in args[1:]]
     return pl.pallas_call(
         kernel,
         out_shape=pltpu.VMEM(shape, jnp.float32) if keep else jax.ShapeDtypeStruct(shape, jnp.float32),
         in_specs=specs,
         out_specs=vmem,
         scratch_shapes=list(scratch_shapes),
+        input_output_aliases=aliases or {},
         cost_estimate=pl.CostEstimate(flops=flops, bytes_accessed=4 * math.prod(shape), transcendentals=0),
         compiler_params=pltpu.CompilerParams(vmem_limit_bytes=24 * 2**20),
     )(*args)
+
+
+def first_call(rows, place, field, mask, link, speed, matrix, dtau):
+    vmem = pl.BlockSpec(memory_space=pltpu.VMEM)
+    given = (mask, link, speed, matrix, dtau)
+    sources = [pltpu.with_memory_space_constraint(a, pltpu.HBM) for a in (field, *given)]
+    outs = [pltpu.VMEM(a.shape, a.dtype) for a in given] + [pltpu.VMEM((rows, dtau.shape[2]), jnp.float32)]
+    return pl.pallas_call(
+        first_kernel,
+        out_shape=outs,
+        in_specs=[pl.BlockSpec(memory_space=pltpu.SMEM)] + [pl.BlockSpec(memory_space=pltpu.HBM)] * 6,
+        out_specs=[vmem] * 6,
+        scratch_shapes=[
+            *scratch(*mask.shape[1:]),
+            pltpu.VMEM(field.shape, jnp.float32),
+            pltpu.SemaphoreType.DMA((6,)),
+        ],
+        cost_estimate=pl.CostEstimate(flops=10**8, bytes_accessed=10**6, transcendentals=0),
+        compiler_params=pltpu.CompilerParams(vmem_limit_bytes=24 * 2**20),
+    )(place, *sources)
 
 
 def shards(matrix, state, frame_velocity, dtau, live_mask, link):
@@ -299,10 +336,8 @@
     flaps, gusts = lax.axis_size("flap"), lax.axis_size("gust")
     count = flaps * gusts
     field = state[0, 0]
-    speed = frame_velocity[0, 0]
-    link = link[None]
-    first = jnp.where(lax.axis_index("span") == 0, 1, 0).astype(jnp.int32)[None]
-    chunk = (lax.axis_index("flap") * gusts + lax.axis_index("gust")).astype(jnp.int32)[None]
+    first = jnp.where(lax.axis_index("span") == 0, 1, 0)
+    place = jnp.stack([first, lax.axis_index("flap") * gusts + lax.axis_index("gust")]).astype(jnp.int32)
     swap = [(0, 1), (1, 0)]
 
     def turn(x):
@@ -312,21 +347,21 @@
     with jax.named_scope("halo"):
         other = lax.ppermute(field, "span", swap)
     with jax.named_scope("first_divergence"):
-        div = call(first_kernel, field.shape, (first, speed, field, live_mask, link), 2, scratch(nj, ni), 10**8)
-        pack = call(first_edge_kernel, (count * 4, ni), (first, speed, field, other, div), 2)
+        mask, link, speed, matrix, dtau, pack = first_call(
+            count * 4, place, field, live_mask, link[None], frame_velocity[0], matrix, dtau
+        )
+        pack = call(first_edge_kernel, pack.shape, (place, speed, other, pack), aliases={3: 0})
     with jax.named_scope("turn"):
         pack = turn(pack)
     with jax.named_scope("instances"):
-        pack = call(instances_kernel, (count * 4, ni), (chunk, matrix, pack, dtau, live_mask), 1, (), 10**8)
+        pack = call(instances_kernel, pack.shape, (place, matrix, pack, dtau, mask), (), 10**8)
     with jax.named_scope("turn_back"):
         pack = turn(pack)
     with jax.named_scope("halo"):
-        other = lax.ppermute(call(edge_kernel, (5, nj, ni), (first, pack), 1), "span", swap)
+        other = lax.ppermute(call(edge_kernel, (5, nj, ni), (place, pack)), "span", swap)
     with jax.named_scope("last_divergence"):
-        residual = call(last_kernel, field.shape, (first, speed, pack, live_mask, link), 2, scratch(nj, ni), 10**8)
-        out = call(
-            last_edge_kernel, field.shape, (first, speed, pack, other, residual, live_mask, dtau), 2, keep=False
-        )
+        residual = call(last_kernel, field.shape, (place, speed, pack, mask, link), scratch(nj, ni), 10**8)
+        out = call(last_edge_kernel, field.shape, (place, speed, pack, other, residual, mask, dtau), keep=False)
     return out[None, None]
 
 

time: 89.3 us -> 88.2 us (0.988)
  blocking collectives: 27.5 us -> 63.4 us
  waiting for transfers between devices: 18.9 us -> 0.01 us
  starting transfers between devices: 31.5 us -> 14.2 us
  local copies, waits for them, and re-layouts: 2.41 us -> 0 us
  Pallas kernels: 8.59 us -> 10.2 us
    all_to_all x1 -> x2, blocking collectives: 27.5 us -> 63.4 us  [turn(): lax.all_to_all(x.reshape(count, 4, ni), ('flap', 'gust'), 0, 0, tiled=True)]
    all_to_all x1 -> x0, waiting for transfers between devices: 18.9 us -> none  [turn(): lax.all_to_all(x.reshape(count, 4, ni), ('flap', 'gust'), 0, 0, tiled=True)]
    all_to_all x1 -> x0, starting transfers between devices: 17.1 us -> none  [turn(): lax.all_to_all(x.reshape(count, 4, ni), ('flap', 'gust'), 0, 0, tiled=True)]
    pallas_call x0 -> x1, Pallas kernels: none -> 3.32 us  [first_call(): pl.pallas_call(first_kernel, out_shape=outs, in_specs=[pl.BlockSpec(memor...]
    unnamed x14 -> x0, local copies, waits for them, and re-layouts: 2.41 us -> none
    pallas_call x6 -> x5, Pallas kernels: 8.59 us -> 6.92 us  [call(): pl.pallas_call(kernel, out_shape=pltpu.VMEM(shape, jnp.float32) if keep e...]
  transfers between devices with their start and end apart: 3 -> 2, of which waited for: 1 -> 0; matrix products, arithmetic and copies ran while one was open for 0% -> 0% of each run, Pallas kernels for 5% -> 6%
where the time goes in v3:
time: 88.2 us; the launch traced here: 87.9 us
  blocking collectives  63.4 us (72%)
  starting transfers between devices  14.2 us (16%)
  Pallas kernels  10.2 us (12%)
    all_to_all x2, blocking collectives, turn(): lax.all_to_all(x.reshape(count, 4, ni), ('flap', 'gust'), 0, 0, tiled=True)  63.4 us
    ppermute x1, starting transfers between devices, shards(): other = lax.ppermute(field, 'span', swap)  8.78 us
    pallas_call x5, Pallas kernels, call(): pl.pallas_call(kernel, out_shape=pltpu.VMEM(shape, jnp.float32) if keep e...  6.92 us
    ppermute x1, starting transfers between devices, shards(): lax.ppermute(call(edge_kernel, (5, nj, ni), (place, pack)), 'span', swap)  5.41 us
    pallas_call x1, Pallas kernels, first_call(): pl.pallas_call(first_kernel, out_shape=outs, in_specs=[pl.BlockSpec(memor...  3.32 us
  transfers between devices with their start and end apart: 2, of which 0 were waited for; matrix products, arithmetic and copies ran while one was open for 0% of the time, Pallas kernels for 6%

profile of v3, /device:TPU:1, one launch (start us, length us, event | category | flops | bytes accessed | tf_op | source)
XLA Modules:
  0.0 87.9 jit_solution(7439533358955436216)
XLA Ops:
  0.0 8.8 %collective-permute-start = (f32[5,2,48,128]{3,2,1,0:T(8,128)}, f32[5,2,48,128]{3,2,1,0:T(8,128)S(1)}, u32[]{:S(2)}, u32[]{:S(2)}) collective-permute-start(f32[5,2,48,128]{3,2,1,0:T(8,128)} %bitcast.16), channel_id=1, source_target_pairs={{0,1},{1,0},{2,3},{3,2},{4,5},{5,4},{6,7},{7,6},{8,9},{9,8},{10,11... | collective-permute-start | bytes 737288 | tf_op jit(solution)/shard_map/halo/ppermute | solution.py:348
  8.8 0.1 pad_add_fusion.place_ref
  8.9 3.3 %first_divergence.2 = (s32[2,48,128]{2,1,0:T(8,128)S(1)}, s32[1,128]{1,0:T(1,128)S(1)}, f32[1,3]{1,0:T(1,128)S(1)}, f32[256,256]{1,0:T(8,128)S(1)}, f32[2,48,128]{2,1,0:T(8,128)S(1)}, /*index=5*/f32[1024,128]{1,0:T(8,128)S(1)}) custom-call(s32[2]{0:T(128)S(1)} %pad_add_fusion.place_ref, f32[5,2,48,128]{3,2,1,0:T(8,128)} %bitcast.17, s32[2,48,128]{2,1,0:T(8,128)} %refs_1_.1, ...), custom_call_target="tpu_custom_call" | custom-call | flops 100000000 | bytes 1000000 | tf_op jit(solution)/shard_map/first_divergence/pallas_call | solution.py:319
  12.2 0.0 collective-permute-done.other_ref
  12.2 1.0 %first_divergence.3 = f32[1024,128]{1,0:T(8,128)S(1)} custom-call(s32[2]{0:T(128)S(1)} %pad_add_fusion.place_ref, f32[1,3]{1,0:T(1,128)S(1)} %get-tuple-element.11.speed_ref, f32[5,2,48,128]{3,2,1,0:T(8,128)S(1)} %collective-permute-done.other_ref, f32[1024,128]{1,0:T(8,128)S(1)} %get-tuple-element.13.pack_ref), custom_call_target="tpu_custom_call", output_to_operand_aliasing={{}: (3, {})} | custom-call | bytes 524288 | tf_op jit(solution)/shard_map/first_divergence/pallas_call | solution.py:302
  13.2 35.7 %all_to_all.10 = f32[256,4,128]{2,1,0:T(4,128)S(1)} all-to-all(f32[256,4,128]{2,1,0:T(4,128)S(1)} %bitcast.15), channel_id=1, replica_groups=mesh['flap'=16,'gust'=16,'span'=2] {'flap','gust'}, dimensions={0} | all-to-all | bytes 1048576 | tf_op jit(solution)/shard_map/turn/all_to_all | solution.py:344
  48.9 1.6 %instances.1 = f32[1024,128]{1,0:T(8,128)S(1)} custom-call(s32[2]{0:T(128)S(1)} %pad_add_fusion.place_ref, f32[256,256]{1,0:T(8,128)S(1)} %get-tuple-element.12.matrix_ref, f32[1024,128]{1,0:T(8,128)S(1)} %bitcast.13, f32[2,48,128]{2,1,0:T(8,128)S(1)} %get-tuple-element.14.dtau_ref, s32[2,48,128]{2,1,0:T(8,128)S(1)} %get-tuple-element.15.mask_ref), custom_call_target="tpu_custom_call" | custom-call | flops 100000000 | bytes 524288 | tf_op jit(solution)/shard_map/instances/pallas_call | solution.py:302
  50.5 27.6 %all_to_all.11 = f32[256,4,128]{2,1,0:T(4,128)S(1)} all-to-all(f32[256,4,128]{2,1,0:T(4,128)S(1)} %bitcast.14), channel_id=1, replica_groups=mesh['flap'=16,'gust'=16,'span'=2] {'flap','gust'}, dimensions={0} | all-to-all | bytes 1048576 | tf_op jit(solution)/shard_map/turn_back/all_to_all | solution.py:344
  78.2 0.6 halo.1
  78.7 5.4 %collective-permute-start.1 = (f32[5,48,128]{2,1,0:T(8,128)S(1)}, f32[5,48,128]{2,1,0:T(8,128)S(1)}, u32[]{:S(2)}, u32[]{:S(2)}) collective-permute-start(f32[5,48,128]{2,1,0:T(8,128)S(1)} %halo.1), channel_id=1, source_target_pairs={{0,1},{1,0},{2,3},{3,2},{4,5},{5,4},{6,7},{7,6},{8,9},{9,8},{10,11... | collective-permute-start | bytes 368648 | tf_op jit(solution)/shard_map/halo/ppermute | solution.py:361
  84.2 2.3 %last_divergence.2.residual_ref = f32[5,2,48,128]{3,2,1,0:T(8,128)S(1)} custom-call(s32[2]{0:T(128)S(1)} %pad_add_fusion.place_ref, f32[1,3]{1,0:T(1,128)S(1)} %get-tuple-element.11.speed_ref, f32[1024,128]{1,0:T(8,128)S(1)} %bitcast.11, s32[2,48,128]{2,1,0:T(8,128)S(1)} %get-tuple-element.15.mask_ref, s32[1,128]{1,0:T(1,128)S(1)} %get-tuple-element.16.link_ref), custom_call_target="tpu_custom_call" | custom-call | flops 100000000 | bytes 245760 | tf_op jit(solution)/shard_map/last_divergence/pallas_call | solution.py:302
  86.5 0.0 collective-permute-done.1.other_ref
  86.5 1.4 %last_divergence.3 = f32[5,2,48,128]{3,2,1,0:T(8,128)} custom-call(s32[2]{0:T(128)S(1)} %pad_add_fusion.place_ref, f32[1,3]{1,0:T(1,128)S(1)} %get-tuple-element.11.speed_ref, f32[1024,128]{1,0:T(8,128)S(1)} %bitcast.12, f32[5,48,128]{2,1,0:T(8,128)S(1)} %collective-permute-done.1.other_ref, f32[5,2,48,128]{3,2,1,0:T(8,128)S(1)} %last_divergence.2.residual_ref, ...), custom_call_target="tpu_custom_call" | custom-call | bytes 245760 | tf_op jit(solution)/shard_map/last_divergence/pallas_call | solution.py:302
Async XLA Ops:
  0.0 12.2 %collective-permute-start = (f32[5,2,48,128]{3,2,1,0:T(8,128)}, f32[5,2,48,128]{3,2,1,0:T(8,128)S(1)}, u32[]{:S(2)}, u32[]{:S(2)}) collective-permute-start(f32[5,2,48,128]{3,2,1,0:T(8,128)} %bitcast.16), channel_id=1, source_target_pairs={{0,1},{1,0},{2,3},{3,2},{4,5},{5,4},{6,7},{7,6},{8,9},{9,8},{10,11... | collective-permute-start | bytes 737288 | tf_op jit(solution)/shard_map/halo/ppermute | solution.py:348
  78.7 7.8 %collective-permute-start.1 = (f32[5,48,128]{2,1,0:T(8,128)S(1)}, f32[5,48,128]{2,1,0:T(8,128)S(1)}, u32[]{:S(2)}, u32[]{:S(2)}) collective-permute-start(f32[5,48,128]{2,1,0:T(8,128)S(1)} %halo.1), channel_id=1, source_target_pairs={{0,1},{1,0},{2,3},{3,2},{4,5},{5,4},{6,7},{7,6},{8,9},{9,8},{10,11... | collective-permute-start | bytes 368648 | tf_op jit(solution)/shard_map/halo/ppermute | solution.py:361

commit v4 on v3

--- a/solution.py
+++ b/solution.py
@@ -127,7 +127,7 @@
             cells[LIVE, k, pl.ds(PAD + row, 8), :] = live
         return carry
 
-    lax.fori_loop(0, blocks, fill, 0)
+    lax.fori_loop(0, blocks, fill, 0, unroll=True)
     link = jnp.broadcast_to(link_ref[...], (8, link_ref.shape[1]))
     for k in range(2):
         for f in range(8):
@@ -149,7 +149,7 @@
                 faces[f, k, pl.ds(row, 8), :] = flux[f]
         return carry
 
-    lax.fori_loop(0, blocks + 1, normal, 0)
+    lax.fori_loop(0, blocks + 1, normal, 0, unroll=True)
 
     def rest(b, carry):
         row = rows(b)
@@ -171,7 +171,7 @@
                 emit(f, k, row, span + after)
         return carry
 
-    lax.fori_loop(0, blocks, rest, 0)
+    lax.fori_loop(0, blocks, rest, 0, unroll=True)
 
 
 def outer_face(mine, other, speed_ref, first):
@@ -193,7 +193,7 @@
     return pl.ds(4 * (f * nj + row) + q, 8, stride=4)
 
 
-def first_kernel(place_ref, *refs):
+def first_kernel(place_ref, chunk_ref, *refs):
     sources, targets, (out_ref, cells, faces, state_ref, sems) = refs[:6], refs[6:11], refs[11:]
     mask_ref, link_ref, speed_ref = targets[:3]
     nj = mask_ref.shape[1]
@@ -273,10 +273,10 @@
             out_ref[f, pl.ds(row, 8), :] = turned_ref[packed(f, row, place_ref[0], nj), :]
 
 
-def instances_kernel(place_ref, matrix_ref, turned_ref, dtau_ref, mask_ref, out_ref):
+def instances_kernel(chunk_ref, matrix_ref, turned_ref, dtau_ref, mask_ref, out_ref):
     count = matrix_ref.shape[0]
     nj = mask_ref.shape[1]
-    j = lax.rem(place_ref[1], nj)
+    j = lax.rem(chunk_ref[0], nj)
     parts = [turned_ref[pl.ds(q, count, stride=4), :] for q in range(4)]
     state = jnp.concatenate(parts[:2], axis=1)
     div = jnp.concatenate(parts[2:], axis=1)
@@ -311,7 +311,7 @@
     )(*args)
 
 
-def first_call(rows, place, field, mask, link, speed, matrix, dtau):
+def first_call(rows, place, chunk, field, mask, link, speed, matrix, dtau):
     vmem = pl.BlockSpec(memory_space=pltpu.VMEM)
     given = (mask, link, speed, matrix, dtau)
     sources = [pltpu.with_memory_space_constraint(a, pltpu.HBM) for a in (field, *given)]
@@ -319,7 +319,7 @@
     return pl.pallas_call(
         first_kernel,
         out_shape=outs,
-        in_specs=[pl.BlockSpec(memory_space=pltpu.SMEM)] + [pl.BlockSpec(memory_space=pltpu.HBM)] * 6,
+        in_specs=[pl.BlockSpec(memory_space=pltpu.SMEM)] * 2 + [pl.BlockSpec(memory_space=pltpu.HBM)] * 6,
         out_specs=[vmem] * 6,
         scratch_shapes=[
             *scratch(*mask.shape[1:]),
@@ -328,7 +328,7 @@
         ],
         cost_estimate=pl.CostEstimate(flops=10**8, bytes_accessed=10**6, transcendentals=0),
         compiler_params=pltpu.CompilerParams(vmem_limit_bytes=24 * 2**20),
-    )(place, *sources)
+    )(place, chunk, *sources)
 
 
 def shards(matrix, state, frame_velocity, dtau, live_mask, link):
@@ -336,8 +336,8 @@
     flaps, gusts = lax.axis_size("flap"), lax.axis_size("gust")
     count = flaps * gusts
     field = state[0, 0]
-    first = jnp.where(lax.axis_index("span") == 0, 1, 0)
-    place = jnp.stack([first, lax.axis_index("flap") * gusts + lax.axis_index("gust")]).astype(jnp.int32)
+    first = jnp.where(lax.axis_index("span") == 0, 1, 0).astype(jnp.int32)[None]
+    chunk = (lax.axis_index("flap") * gusts + lax.axis_index("gust")).astype(jnp.int32)[None]
     swap = [(0, 1), (1, 0)]
 
     def turn(x):
@@ -348,20 +348,20 @@
         other = lax.ppermute(field, "span", swap)
     with jax.named_scope("first_divergence"):
         mask, link, speed, matrix, dtau, pack = first_call(
-            count * 4, place, field, live_mask, link[None], frame_velocity[0], matrix, dtau
+            count * 4, first, chunk, field, live_mask, link[None], frame_velocity[0], matrix, dtau
         )
-        pack = call(first_edge_kernel, pack.shape, (place, speed, other, pack), aliases={3: 0})
+        pack = call(first_edge_kernel, pack.shape, (first, speed, other, pack), aliases={3: 0})
     with jax.named_scope("turn"):
         pack = turn(pack)
     with jax.named_scope("instances"):
-        pack = call(instances_kernel, pack.shape, (place, matrix, pack, dtau, mask), (), 10**8)
+        pack = call(instances_kernel, pack.shape, (chunk, matrix, pack, dtau, mask), (), 10**8)
     with jax.named_scope("turn_back"):
         pack = turn(pack)
     with jax.named_scope("halo"):
-        other = lax.ppermute(call(edge_kernel, (5, nj, ni), (place, pack)), "span", swap)
+        other = lax.ppermute(call(edge_kernel, (5, nj, ni), (first, pack)), "span", swap)
     with jax.named_scope("last_divergence"):
-        residual = call(last_kernel, field.shape, (place, speed, pack, mask, link), scratch(nj, ni), 10**8)
-        out = call(last_edge_kernel, field.shape, (place, speed, pack, other, residual, mask, dtau), keep=False)
+        residual = call(last_kernel, field.shape, (first, speed, pack, mask, link), scratch(nj, ni), 10**8)
+        out = call(last_edge_kernel, field.shape, (first, speed, pack, other, residual, mask, dtau), keep=False)
     return out[None, None]
 
 

time: 88.2 us -> 83.1 us (0.942)
  Pallas kernels: 10.2 us -> 5.09 us
    pallas_call x5, Pallas kernels: 6.92 us -> 3.25 us  [call(): pl.pallas_call(kernel, out_shape=pltpu.VMEM(shape, jnp.float32) if keep e...]
    pallas_call x1, Pallas kernels: 3.32 us -> 1.85 us  [first_call(): pl.pallas_call(first_kernel, out_shape=outs, in_specs=[pl.BlockSpec(memor...]
  transfers between devices with their start and end apart: 2 -> 2, of which waited for: 0 -> 1; matrix products, arithmetic and copies ran while one was open for 0% -> 0% of each run, Pallas kernels for 6% -> 3%
where the time goes in v4:
time: 83.1 us; the launch traced here: 82.8 us
  blocking collectives  63.4 us (76%)
  starting transfers between devices  14.2 us (17%)
  Pallas kernels  5.09 us (6%)
    all_to_all x2, blocking collectives, turn(): lax.all_to_all(x.reshape(count, 4, ni), ('flap', 'gust'), 0, 0, tiled=True)  63.4 us
    ppermute x1, starting transfers between devices, shards(): other = lax.ppermute(field, 'span', swap)  8.77 us
    ppermute x1, starting transfers between devices, shards(): lax.ppermute(call(edge_kernel, (5, nj, ni), (first, pack)), 'span', swap)  5.41 us
    pallas_call x5, Pallas kernels, call(): pl.pallas_call(kernel, out_shape=pltpu.VMEM(shape, jnp.float32) if keep e...  3.25 us
    pallas_call x1, Pallas kernels, first_call(): pl.pallas_call(first_kernel, out_shape=outs, in_specs=[pl.BlockSpec(memor...  1.85 us
  transfers between devices with their start and end apart: 2, of which 1 were waited for; matrix products, arithmetic and copies ran while one was open for 0% of the time, Pallas kernels for 3%

profile of v4, /device:TPU:1, one launch (start us, length us, event | category | flops | bytes accessed | tf_op | source)
XLA Modules:
  0.0 82.8 jit_solution(192990675183778826)
XLA Ops:
  0.0 8.8 %collective-permute-start = (f32[5,2,48,128]{3,2,1,0:T(8,128)}, f32[5,2,48,128]{3,2,1,0:T(8,128)S(1)}, u32[]{:S(2)}, u32[]{:S(2)}) collective-permute-start(f32[5,2,48,128]{3,2,1,0:T(8,128)} %bitcast.16), channel_id=1, source_target_pairs={{0,1},{1,0},{2,3},{3,2},{4,5},{5,4},{6,7},{7,6},{8,9},{9,8},{10,11... | collective-permute-start | bytes 737288 | tf_op jit(solution)/shard_map/halo/ppermute | solution.py:348
  8.8 1.8 %first_divergence.2 = (s32[2,48,128]{2,1,0:T(8,128)S(1)}, s32[1,128]{1,0:T(1,128)S(1)}, f32[1,3]{1,0:T(1,128)S(1)}, f32[256,256]{1,0:T(8,128)S(1)}, f32[2,48,128]{2,1,0:T(8,128)S(1)}, /*index=5*/f32[1024,128]{1,0:T(8,128)S(1)}) custom-call(s32[1]{0:T(128)} %bitcast.place_ref, s32[1]{0:T(128)} %bitcast.1.chunk_ref, f32[5,2,48,128]{3,2,1,0:T(8,128)} %bitcast.17, ...), custom_call_target="tpu_custom_call" | custom-call | flops 100000000 | bytes 1000000 | tf_op jit(solution)/shard_map/first_divergence/pallas_call | solution.py:319
  10.6 0.0 collective-permute-done.other_ref
  10.7 0.4 first_divergence.3
  11.1 35.7 %all_to_all.10 = f32[256,4,128]{2,1,0:T(4,128)S(1)} all-to-all(f32[256,4,128]{2,1,0:T(4,128)S(1)} %bitcast.15), channel_id=1, replica_groups=mesh['flap'=16,'gust'=16,'span'=2] {'flap','gust'}, dimensions={0} | all-to-all | bytes 1048576 | tf_op jit(solution)/shard_map/turn/all_to_all | solution.py:344
  46.8 1.1 %instances.1 = f32[1024,128]{1,0:T(8,128)S(1)} custom-call(s32[1]{0:T(128)} %bitcast.1.chunk_ref, f32[256,256]{1,0:T(8,128)S(1)} %get-tuple-element.12.matrix_ref, f32[1024,128]{1,0:T(8,128)S(1)} %bitcast.13, f32[2,48,128]{2,1,0:T(8,128)S(1)} %get-tuple-element.14.dtau_ref, s32[2,48,128]{2,1,0:T(8,128)S(1)} %get-tuple-element.15.mask_ref), custom_call_target="tpu_custom_call" | custom-call | flops 100000000 | bytes 524288 | tf_op jit(solution)/shard_map/instances/pallas_call | solution.py:302
  47.9 27.6 %all_to_all.11 = f32[256,4,128]{2,1,0:T(4,128)S(1)} all-to-all(f32[256,4,128]{2,1,0:T(4,128)S(1)} %bitcast.14), channel_id=1, replica_groups=mesh['flap'=16,'gust'=16,'span'=2] {'flap','gust'}, dimensions={0} | all-to-all | bytes 1048576 | tf_op jit(solution)/shard_map/turn_back/all_to_all | solution.py:344
  75.6 5.4 %collective-permute-start.1 = (f32[5,48,128]{2,1,0:T(8,128)S(1)}, f32[5,48,128]{2,1,0:T(8,128)S(1)}, u32[]{:S(2)}, u32[]{:S(2)}) collective-permute-start(f32[5,48,128]{2,1,0:T(8,128)S(1)} %halo.1), channel_id=1, source_target_pairs={{0,1},{1,0},{2,3},{3,2},{4,5},{5,4},{6,7},{7,6},{8,9},{9,8},{10,11... | collective-permute-start | bytes 368648 | tf_op jit(solution)/shard_map/halo/ppermute | solution.py:361
  81.0 0.8 last_divergence.2.residual_ref
  81.8 0.1 collective-permute-done.1.other_ref
  81.9 0.9 %last_divergence.3 = f32[5,2,48,128]{3,2,1,0:T(8,128)} custom-call(s32[1]{0:T(128)} %bitcast.place_ref, f32[1,3]{1,0:T(1,128)S(1)} %get-tuple-element.11.speed_ref, f32[1024,128]{1,0:T(8,128)S(1)} %bitcast.12, f32[5,48,128]{2,1,0:T(8,128)S(1)} %collective-permute-done.1.other_ref, f32[5,2,48,128]{3,2,1,0:T(8,128)S(1)} %last_divergence.2.residual_ref, ...), custom_call_target="tpu_custom_call" | custom-call | bytes 245760 | tf_op jit(solution)/shard_map/last_divergence/pallas_call | solution.py:302
  (1 shorter events, 0.0 us)
Async XLA Ops:
  0.0 10.7 %collective-permute-start = (f32[5,2,48,128]{3,2,1,0:T(8,128)}, f32[5,2,48,128]{3,2,1,0:T(8,128)S(1)}, u32[]{:S(2)}, u32[]{:S(2)}) collective-permute-start(f32[5,2,48,128]{3,2,1,0:T(8,128)} %bitcast.16), channel_id=1, source_target_pairs={{0,1},{1,0},{2,3},{3,2},{4,5},{5,4},{6,7},{7,6},{8,9},{9,8},{10,11... | collective-permute-start | bytes 737288 | tf_op jit(solution)/shard_map/halo/ppermute | solution.py:348
  75.6 6.4 %collective-permute-start.1 = (f32[5,48,128]{2,1,0:T(8,128)S(1)}, f32[5,48,128]{2,1,0:T(8,128)S(1)}, u32[]{:S(2)}, u32[]{:S(2)}) collective-permute-start(f32[5,48,128]{2,1,0:T(8,128)S(1)} %halo.1), channel_id=1, source_target_pairs={{0,1},{1,0},{2,3},{3,2},{4,5},{5,4},{6,7},{7,6},{8,9},{9,8},{10,11... | collective-permute-start | bytes 368648 | tf_op jit(solution)/shard_map/halo/ppermute | solution.py:361

commit v5 on v4

--- a/solution.py
+++ b/solution.py
@@ -285,7 +285,7 @@
     matrix = matrix_ref[...]
 
     def times(x):
-        return jnp.dot(matrix, x, precision=lax.Precision.HIGHEST, preferred_element_type=jnp.float32)
+        return jnp.dot(matrix, x, precision=lax.Precision.HIGH, preferred_element_type=jnp.float32)
 
     new = state - dtau * (div + times(state))
     new = jnp.where(mask > 0, new, state)

time: 83.1 us -> 82.7 us (level)
  no operation moved by 1% of the time
where the time goes in v5:
time: 82.7 us; the launch traced here: 82.4 us
  blocking collectives  63.4 us (77%)
  starting transfers between devices  14.2 us (17%)
  Pallas kernels  4.68 us (6%)
    all_to_all x2, blocking collectives, turn(): lax.all_to_all(x.reshape(count, 4, ni), ('flap', 'gust'), 0, 0, tiled=True)  63.4 us
    ppermute x1, starting transfers between devices, shards(): other = lax.ppermute(field, 'span', swap)  8.77 us
    ppermute x1, starting transfers between devices, shards(): lax.ppermute(call(edge_kernel, (5, nj, ni), (first, pack)), 'span', swap)  5.41 us
    pallas_call x5, Pallas kernels, call(): pl.pallas_call(kernel, out_shape=pltpu.VMEM(shape, jnp.float32) if keep e...  2.83 us
    pallas_call x1, Pallas kernels, first_call(): pl.pallas_call(first_kernel, out_shape=outs, in_specs=[pl.BlockSpec(memor...  1.85 us
  transfers between devices with their start and end apart: 2, of which 1 were waited for; matrix products, arithmetic and copies ran while one was open for 0% of the time, Pallas kernels for 3%

profile of v5, /device:TPU:1, one launch (start us, length us, event | category | flops | bytes accessed | tf_op | source)
XLA Modules:
  0.0 82.4 jit_solution(15365432358998538191)
XLA Ops:
  0.0 8.8 %collective-permute-start = (f32[5,2,48,128]{3,2,1,0:T(8,128)}, f32[5,2,48,128]{3,2,1,0:T(8,128)S(1)}, u32[]{:S(2)}, u32[]{:S(2)}) collective-permute-start(f32[5,2,48,128]{3,2,1,0:T(8,128)} %bitcast.16), channel_id=1, source_target_pairs={{0,1},{1,0},{2,3},{3,2},{4,5},{5,4},{6,7},{7,6},{8,9},{9,8},{10,11... | collective-permute-start | bytes 737288 | tf_op jit(solution)/shard_map/halo/ppermute | solution.py:348
  8.8 1.8 %first_divergence.2 = (s32[2,48,128]{2,1,0:T(8,128)S(1)}, s32[1,128]{1,0:T(1,128)S(1)}, f32[1,3]{1,0:T(1,128)S(1)}, f32[256,256]{1,0:T(8,128)S(1)}, f32[2,48,128]{2,1,0:T(8,128)S(1)}, /*index=5*/f32[1024,128]{1,0:T(8,128)S(1)}) custom-call(s32[1]{0:T(128)} %bitcast.place_ref, s32[1]{0:T(128)} %bitcast.1.chunk_ref, f32[5,2,48,128]{3,2,1,0:T(8,128)} %bitcast.17, ...), custom_call_target="tpu_custom_call" | custom-call | flops 100000000 | bytes 1000000 | tf_op jit(solution)/shard_map/first_divergence/pallas_call | solution.py:319
  10.6 0.0 collective-permute-done.other_ref
  10.7 0.4 first_divergence.3
  11.1 35.7 %all_to_all.10 = f32[256,4,128]{2,1,0:T(4,128)S(1)} all-to-all(f32[256,4,128]{2,1,0:T(4,128)S(1)} %bitcast.15), channel_id=1, replica_groups=mesh['flap'=16,'gust'=16,'span'=2] {'flap','gust'}, dimensions={0} | all-to-all | bytes 1048576 | tf_op jit(solution)/shard_map/turn/all_to_all | solution.py:344
  46.8 0.7 instances.1
  47.5 27.7 %all_to_all.11 = f32[256,4,128]{2,1,0:T(4,128)S(1)} all-to-all(f32[256,4,128]{2,1,0:T(4,128)S(1)} %bitcast.14), channel_id=1, replica_groups=mesh['flap'=16,'gust'=16,'span'=2] {'flap','gust'}, dimensions={0} | all-to-all | bytes 1048576 | tf_op jit(solution)/shard_map/turn_back/all_to_all | solution.py:344
  75.1 5.4 %collective-permute-start.1 = (f32[5,48,128]{2,1,0:T(8,128)S(1)}, f32[5,48,128]{2,1,0:T(8,128)S(1)}, u32[]{:S(2)}, u32[]{:S(2)}) collective-permute-start(f32[5,48,128]{2,1,0:T(8,128)S(1)} %halo.1), channel_id=1, source_target_pairs={{0,1},{1,0},{2,3},{3,2},{4,5},{5,4},{6,7},{7,6},{8,9},{9,8},{10,11... | collective-permute-start | bytes 368648 | tf_op jit(solution)/shard_map/halo/ppermute | solution.py:361
  80.6 0.8 %last_divergence.2.residual_ref = f32[5,2,48,128]{3,2,1,0:T(8,128)S(1)} custom-call(s32[1]{0:T(128)} %bitcast.place_ref, f32[1,3]{1,0:T(1,128)S(1)} %get-tuple-element.11.speed_ref, f32[1024,128]{1,0:T(8,128)S(1)} %bitcast.11, s32[2,48,128]{2,1,0:T(8,128)S(1)} %get-tuple-element.15.mask_ref, s32[1,128]{1,0:T(1,128)S(1)} %get-tuple-element.16.link_ref), custom_call_target="tpu_custom_call" | custom-call | flops 100000000 | bytes 245760 | tf_op jit(solution)/shard_map/last_divergence/pallas_call | solution.py:302
  81.4 0.1 collective-permute-done.1.other_ref
  81.5 0.9 %last_divergence.3 = f32[5,2,48,128]{3,2,1,0:T(8,128)} custom-call(s32[1]{0:T(128)} %bitcast.place_ref, f32[1,3]{1,0:T(1,128)S(1)} %get-tuple-element.11.speed_ref, f32[1024,128]{1,0:T(8,128)S(1)} %bitcast.12, f32[5,48,128]{2,1,0:T(8,128)S(1)} %collective-permute-done.1.other_ref, f32[5,2,48,128]{3,2,1,0:T(8,128)S(1)} %last_divergence.2.residual_ref, ...), custom_call_target="tpu_custom_call" | custom-call | bytes 245760 | tf_op jit(solution)/shard_map/last_divergence/pallas_call | solution.py:302
  (1 shorter events, 0.0 us)
Async XLA Ops:
  0.0 10.7 %collective-permute-start = (f32[5,2,48,128]{3,2,1,0:T(8,128)}, f32[5,2,48,128]{3,2,1,0:T(8,128)S(1)}, u32[]{:S(2)}, u32[]{:S(2)}) collective-permute-start(f32[5,2,48,128]{3,2,1,0:T(8,128)} %bitcast.16), channel_id=1, source_target_pairs={{0,1},{1,0},{2,3},{3,2},{4,5},{5,4},{6,7},{7,6},{8,9},{9,8},{10,11... | collective-permute-start | bytes 737288 | tf_op jit(solution)/shard_map/halo/ppermute | solution.py:348
  75.1 6.4 %collective-permute-start.1 = (f32[5,48,128]{2,1,0:T(8,128)S(1)}, f32[5,48,128]{2,1,0:T(8,128)S(1)}, u32[]{:S(2)}, u32[]{:S(2)}) collective-permute-start(f32[5,48,128]{2,1,0:T(8,128)S(1)} %halo.1), channel_id=1, source_target_pairs={{0,1},{1,0},{2,3},{3,2},{4,5},{5,4},{6,7},{7,6},{8,9},{9,8},{10,11... | collective-permute-start | bytes 368648 | tf_op jit(solution)/shard_map/halo/ppermute | solution.py:361

commit v6 on v5

--- a/solution.py
+++ b/solution.py
@@ -175,7 +175,7 @@
 
 
 def outer_face(mine, other, speed_ref, first):
-    mine, other = primitives(*mine), primitives(*other)
+    other = primitives(*other)
     left = [jnp.where(first, a, b) for a, b in zip(mine, other)]
     right = [jnp.where(first, b, a) for a, b in zip(mine, other)]
     sign = jnp.where(first, 1.0, -1.0)
@@ -194,7 +194,7 @@
 
 
 def first_kernel(place_ref, chunk_ref, *refs):
-    sources, targets, (out_ref, cells, faces, state_ref, sems) = refs[:6], refs[6:11], refs[11:]
+    sources, targets, (out_ref, near_ref, cells, faces, state_ref, sems) = refs[:6], refs[6:11], refs[11:]
     mask_ref, link_ref, speed_ref = targets[:3]
     nj = mask_ref.shape[1]
     copies = [
@@ -217,16 +217,17 @@
         out_ref[packed(f, row, 2 + k, nj), :] = div
 
     most_of_divergence(load, mask_ref, link_ref, speed_ref, place_ref[0] > 0, cells, faces, emit)
+    near_ref[...] = cells[:LIVE, place_ref[0], PAD : PAD + nj, :]
     for copy in copies[4:]:
         copy.wait()
 
 
-def first_edge_kernel(place_ref, speed_ref, other_ref, pack_ref, out_ref):
+def first_edge_kernel(place_ref, speed_ref, near_ref, other_ref, pack_ref, out_ref):
     nj = other_ref.shape[2]
     edge = place_ref[0]
     out_ref[...] = pack_ref[...]
     for row in range(0, nj, 8):
-        mine = [pack_ref[packed(f, row, edge, nj), :] for f in range(5)]
+        mine = [near_ref[f, pl.ds(row, 8), :] for f in range(LIVE)]
         other = [other_ref[f, 1 - edge, pl.ds(row, 8), :] for f in range(5)]
         flux = outer_face(mine, other, speed_ref, edge > 0)
         for f in range(5):
@@ -234,36 +235,36 @@
             out_ref[div, :] = pack_ref[div, :] + flux[f]
 
 
-def last_kernel(place_ref, speed_ref, turned_ref, mask_ref, link_ref, out_ref, cells, faces):
+def last_kernel(place_ref, speed_ref, turned_ref, mask_ref, dtau_ref, link_ref, out_ref, near_ref, cells, faces):
     nj = mask_ref.shape[1]
 
     def load(f, k, row):
         return turned_ref[packed(f, row, k, nj), :]
 
     def emit(f, k, row, div):
-        out_ref[f, k, pl.ds(row, 8), :] = div + turned_ref[packed(f, row, 2 + k, nj), :]
+        block = pl.ds(row, 8)
+        old = load(f, k, row)
+        new = old - dtau_ref[k, block, :] * (div + turned_ref[packed(f, row, 2 + k, nj), :])
+        out_ref[f, k, block, :] = jnp.where(mask_ref[k, block, :] > 0, new, old)
 
     most_of_divergence(load, mask_ref, link_ref, speed_ref, place_ref[0] > 0, cells, faces, emit)
-
-
-def last_edge_kernel(place_ref, speed_ref, turned_ref, other_ref, residual_ref, mask_ref, dtau_ref, out_ref):
+    near_ref[...] = cells[:LIVE, place_ref[0], PAD : PAD + nj, :]
+
+
+def last_edge_kernel(place_ref, speed_ref, near_ref, other_ref, most_ref, mask_ref, dtau_ref, out_ref):
     nj = mask_ref.shape[1]
     edge = place_ref[0]
-    first = edge > 0
+    for f in range(5):
+        out_ref[f, 1 - edge, :, :] = most_ref[f, 1 - edge, :, :]
     for row in range(0, nj, 8):
         block = pl.ds(row, 8)
-        mine = [turned_ref[packed(f, row, edge, nj), :] for f in range(5)]
-        flux = outer_face(mine, [other_ref[f, block, :] for f in range(5)], speed_ref, first)
-        for k in (edge, 1 - edge):
-            live = mask_ref[k, block, :] > 0
-            dtau = dtau_ref[k, block, :]
-            for f in range(5):
-                residual = residual_ref[f, k, block, :]
-                if k is edge:
-                    old, residual = mine[f], residual + flux[f]
-                else:
-                    old = turned_ref[packed(f, row, k, nj), :]
-                out_ref[f, k, block, :] = jnp.where(live, old - dtau * residual, old)
+        mine = [near_ref[f, block, :] for f in range(LIVE)]
+        flux = outer_face(mine, [other_ref[f, block, :] for f in range(5)], speed_ref, edge > 0)
+        live = mask_ref[edge, block, :] > 0
+        dtau = dtau_ref[edge, block, :]
+        for f in range(5):
+            most = most_ref[f, edge, block, :]
+            out_ref[f, edge, block, :] = jnp.where(live, most - dtau * flux[f], most)
 
 
 def edge_kernel(place_ref, turned_ref, out_ref):
@@ -295,37 +296,37 @@
         out_ref[pl.ds(q, count, stride=4), :] = value
 
 
-def call(kernel, shape, args, scratch_shapes=(), flops=0, aliases=None, keep=True):
+def call(kernel, shapes, args, scratch_shapes=(), flops=0, aliases=None, keep=True):
     vmem = pl.BlockSpec(memory_space=pltpu.VMEM)
     specs = [pl.BlockSpec(memory_space=pltpu.SMEM)] + [vmem] * (len(args) - 1)
     args = [args[0]] + [pltpu.with_memory_space_constraint(a, pltpu.VMEM) for a in args[1:]]
-    return pl.pallas_call(
+    held = pltpu.VMEM if keep else jax.ShapeDtypeStruct
+    outs = pl.pallas_call(
         kernel,
-        out_shape=pltpu.VMEM(shape, jnp.float32) if keep else jax.ShapeDtypeStruct(shape, jnp.float32),
+        out_shape=[held(shape, jnp.float32) for shape in shapes],
         in_specs=specs,
-        out_specs=vmem,
+        out_specs=[vmem] * len(shapes),
         scratch_shapes=list(scratch_shapes),
         input_output_aliases=aliases or {},
-        cost_estimate=pl.CostEstimate(flops=flops, bytes_accessed=4 * math.prod(shape), transcendentals=0),
+        cost_estimate=pl.CostEstimate(flops=flops, bytes_accessed=10**6, transcendentals=0),
         compiler_params=pltpu.CompilerParams(vmem_limit_bytes=24 * 2**20),
     )(*args)
+    return outs if len(shapes) > 1 else outs[0]
 
 
 def first_call(rows, place, chunk, field, mask, link, speed, matrix, dtau):
     vmem = pl.BlockSpec(memory_space=pltpu.VMEM)
+    nj, ni = mask.shape[1:]
     given = (mask, link, speed, matrix, dtau)
     sources = [pltpu.with_memory_space_constraint(a, pltpu.HBM) for a in (field, *given)]
-    outs = [pltpu.VMEM(a.shape, a.dtype) for a in given] + [pltpu.VMEM((rows, dtau.shape[2]), jnp.float32)]
+    outs = [pltpu.VMEM(a.shape, a.dtype) for a in given]
+    outs += [pltpu.VMEM(shape, jnp.float32) for shape in ((rows, ni), (LIVE, nj, ni))]
     return pl.pallas_call(
         first_kernel,
         out_shape=outs,
         in_specs=[pl.BlockSpec(memory_space=pltpu.SMEM)] * 2 + [pl.BlockSpec(memory_space=pltpu.HBM)] * 6,
-        out_specs=[vmem] * 6,
-        scratch_shapes=[
-            *scratch(*mask.shape[1:]),
-            pltpu.VMEM(field.shape, jnp.float32),
-            pltpu.SemaphoreType.DMA((6,)),
-        ],
+        out_specs=[vmem] * 7,
+        scratch_shapes=[*scratch(nj, ni), pltpu.VMEM(field.shape, jnp.float32), pltpu.SemaphoreType.DMA((6,))],
         cost_estimate=pl.CostEstimate(flops=10**8, bytes_accessed=10**6, transcendentals=0),
         compiler_params=pltpu.CompilerParams(vmem_limit_bytes=24 * 2**20),
     )(place, chunk, *sources)
@@ -347,21 +348,27 @@
     with jax.named_scope("halo"):
         other = lax.ppermute(field, "span", swap)
     with jax.named_scope("first_divergence"):
-        mask, link, speed, matrix, dtau, pack = first_call(
+        mask, link, speed, matrix, dtau, pack, near = first_call(
             count * 4, first, chunk, field, live_mask, link[None], frame_velocity[0], matrix, dtau
         )
-        pack = call(first_edge_kernel, pack.shape, (first, speed, other, pack), aliases={3: 0})
+        pack = call(first_edge_kernel, [pack.shape], (first, speed, near, other, pack), aliases={4: 0})
     with jax.named_scope("turn"):
         pack = turn(pack)
     with jax.named_scope("instances"):
-        pack = call(instances_kernel, pack.shape, (chunk, matrix, pack, dtau, mask), (), 10**8)
+        pack = call(instances_kernel, [pack.shape], (chunk, matrix, pack, dtau, mask), (), 10**8)
     with jax.named_scope("turn_back"):
         pack = turn(pack)
     with jax.named_scope("halo"):
-        other = lax.ppermute(call(edge_kernel, (5, nj, ni), (first, pack)), "span", swap)
+        other = lax.ppermute(call(edge_kernel, [(5, nj, ni)], (first, pack)), "span", swap)
     with jax.named_scope("last_divergence"):
-        residual = call(last_kernel, field.shape, (first, speed, pack, mask, link), scratch(nj, ni), 10**8)
-        out = call(last_edge_kernel, field.shape, (first, speed, pack, other, residual, mask, dtau), keep=False)
+        most, near = call(
+            last_kernel,
+            [field.shape, (LIVE, nj, ni)],
+            (first, speed, pack, mask, dtau, link),
+            scratch(nj, ni),
+            10**8,
+        )
+        out = call(last_edge_kernel, [field.shape], (first, speed, near, other, most, mask, dtau), keep=False)
     return out[None, None]
 
 

time: 82.7 us -> 82.5 us (level)
  no operation moved by 1% of the time
where the time goes in v6:
time: 82.5 us; the launch traced here: 82.2 us
  blocking collectives  63.3 us (77%)
  starting transfers between devices  14.2 us (17%)
  Pallas kernels  4.58 us (6%)
    all_to_all x2, blocking collectives, turn(): lax.all_to_all(x.reshape(count, 4, ni), ('flap', 'gust'), 0, 0, tiled=True)  63.3 us
    ppermute x1, starting transfers between devices, shards(): other = lax.ppermute(field, 'span', swap)  8.77 us
    ppermute x1, starting transfers between devices, shards(): lax.ppermute(call(edge_kernel, [(5, nj, ni)], (first, pack)), 'span', swap)  5.44 us
    pallas_call x5, Pallas kernels, call(): pl.pallas_call(kernel, out_shape=[held(shape, jnp.float32) for shape in s...  2.71 us
    pallas_call x1, Pallas kernels, first_call(): pl.pallas_call(first_kernel, out_shape=outs, in_specs=[pl.BlockSpec(memor...  1.87 us
  transfers between devices with their start and end apart: 2, of which 1 were waited for; matrix products, arithmetic and copies ran while one was open for 0% of the time, Pallas kernels for 3%

profile of v6, /device:TPU:1, one launch (start us, length us, event | category | flops | bytes accessed | tf_op | source)
XLA Modules:
  0.0 82.2 jit_solution(15185648607739073217)
XLA Ops:
  0.0 8.8 %collective-permute-start = (f32[5,2,48,128]{3,2,1,0:T(8,128)}, f32[5,2,48,128]{3,2,1,0:T(8,128)S(1)}, u32[]{:S(2)}, u32[]{:S(2)}) collective-permute-start(f32[5,2,48,128]{3,2,1,0:T(8,128)} %bitcast.15), channel_id=1, source_target_pairs={{0,1},{1,0},{2,3},{3,2},{4,5},{5,4},{6,7},{7,6},{8,9},{9,8},{10,11... | collective-permute-start | bytes 737288 | tf_op jit(solution)/shard_map/halo/ppermute | solution.py:349
  8.8 1.9 %first_divergence.2 = (s32[2,48,128]{2,1,0:T(8,128)S(1)}, s32[1,128]{1,0:T(1,128)S(1)}, f32[1,3]{1,0:T(1,128)S(1)}, f32[256,256]{1,0:T(8,128)S(1)}, f32[2,48,128...) custom-call(s32[1]{0:T(128)} %bitcast.place_ref, s32[1]{0:T(128)} %bitcast.1.chunk_ref, ...), custom_call_target="tpu_custom_call" | custom-call | flops 100000000 | bytes 1000000 | tf_op jit(solution)/shard_map/first_divergence/pallas_call | solution.py:324
  10.7 0.0 collective-permute-done.other_ref
  10.7 0.3 first_divergence.3
  11.0 35.7 %all_to_all.10 = f32[256,4,128]{2,1,0:T(4,128)S(1)} all-to-all(f32[256,4,128]{2,1,0:T(4,128)S(1)} %bitcast.14), channel_id=1, replica_groups=mesh['flap'=16,'gust'=16,'span'=2] {'flap','gust'}, dimensions={0} | all-to-all | bytes 1048576 | tf_op jit(solution)/shard_map/turn/all_to_all | solution.py:345
  46.6 0.7 instances.1
  47.3 27.6 %all_to_all.11 = f32[256,4,128]{2,1,0:T(4,128)S(1)} all-to-all(f32[256,4,128]{2,1,0:T(4,128)S(1)} %bitcast.13), channel_id=1, replica_groups=mesh['flap'=16,'gust'=16,'span'=2] {'flap','gust'}, dimensions={0} | all-to-all | bytes 1048576 | tf_op jit(solution)/shard_map/turn_back/all_to_all | solution.py:345
  75.0 5.4 %collective-permute-start.1 = (f32[5,48,128]{2,1,0:T(8,128)S(1)}, f32[5,48,128]{2,1,0:T(8,128)S(1)}, u32[]{:S(2)}, u32[]{:S(2)}) collective-permute-start(f32[5,48,128]{2,1,0:T(8,128)S(1)} %halo.1), channel_id=1, source_target_pairs={{0,1},{1,0},{2,3},{3,2},{4,5},{5,4},{6,7},{7,6},{8,9},{9,8},{10,11... | collective-permute-start | bytes 368648 | tf_op jit(solution)/shard_map/halo/ppermute | solution.py:362
  80.4 0.9 %last_divergence.2 = (f32[5,2,48,128]{3,2,1,0:T(8,128)S(1)}, f32[7,48,128]{2,1,0:T(8,128)S(1)}) custom-call(s32[1]{0:T(128)} %bitcast.place_ref, f32[1,3]{1,0:T(1,128)S(1)} %get-tuple-element.14.speed_ref, f32[1024,128]{1,0:T(8,128)S(1)} %bitcast.11, s32[2,48,128]{2,1,0:T(8,128)S(1)} %get-tuple-element.19.mask_ref, ...), custom_call_target="tpu_custom_call" | custom-call | flops 100000000 | bytes 1000000 | tf_op jit(solution)/shard_map/last_divergence/pallas_call | solution.py:304
  81.3 0.1 collective-permute-done.1.other_ref
  81.4 0.9 %last_divergence.3 = f32[5,2,48,128]{3,2,1,0:T(8,128)} custom-call(s32[1]{0:T(128)} %bitcast.place_ref, f32[1,3]{1,0:T(1,128)S(1)} %get-tuple-element.14.speed_ref, f32[7,48,128]{2,1,0:T(8,128)S(1)} %get-tuple-element.21.near_ref, f32[5,48,128]{2,1,0:T(8,128)S(1)} %collective-permute-done.1.other_ref, f32[5,2,48,128]{3,2,1,0:T(8,128)S(1)} %get-tuple-element.22.most_ref, ...), custom_call_target="tpu_custom_call" | custom-call | bytes 1000000 | tf_op jit(solution)/shard_map/last_divergence/pallas_call | solution.py:304
  (1 shorter events, 0.0 us)
Async XLA Ops:
  0.0 10.7 %collective-permute-start = (f32[5,2,48,128]{3,2,1,0:T(8,128)}, f32[5,2,48,128]{3,2,1,0:T(8,128)S(1)}, u32[]{:S(2)}, u32[]{:S(2)}) collective-permute-start(f32[5,2,48,128]{3,2,1,0:T(8,128)} %bitcast.15), channel_id=1, source_target_pairs={{0,1},{1,0},{2,3},{3,2},{4,5},{5,4},{6,7},{7,6},{8,9},{9,8},{10,11... | collective-permute-start | bytes 737288 | tf_op jit(solution)/shard_map/halo/ppermute | solution.py:349
  75.0 6.4 %collective-permute-start.1 = (f32[5,48,128]{2,1,0:T(8,128)S(1)}, f32[5,48,128]{2,1,0:T(8,128)S(1)}, u32[]{:S(2)}, u32[]{:S(2)}) collective-permute-start(f32[5,48,128]{2,1,0:T(8,128)S(1)} %halo.1), channel_id=1, source_target_pairs={{0,1},{1,0},{2,3},{3,2},{4,5},{5,4},{6,7},{7,6},{8,9},{9,8},{10,11... | collective-permute-start | bytes 368648 | tf_op jit(solution)/shard_map/halo/ppermute | solution.py:362

commit v7 on v6

--- a/solution.py
+++ b/solution.py
@@ -36,7 +36,7 @@
 
 
 def physical(cell, axis, g):
-    rho, vel, p, enth = cell[RHO], cell[U : W + 1], cell[PR], cell[EN]
+    rho, vel, p, enth = 2.0 * cell[RHO], cell[U : W + 1], 2.0 * cell[PR], cell[EN]
     mass = rho * (vel[axis] - g)
     mom = [mass * vel[a] + p if a == axis else mass * vel[a] for a in range(3)]
     return [mass, *mom, mass * enth + g * p]
@@ -77,17 +77,17 @@
     skew = (w3 - w1) * c
     mass_l = rho_l * (vel_l[axis] - g)
     mass_r = rho_r * (vel_r[axis] - g)
-    out = [0.5 * (mass_l + mass_r - total)]
+    out = [mass_l + mass_r - total]
     for a in range(3):
         flux = mass_l * vel_l[a] + mass_r * vel_r[a]
         if a == axis:
             flux = flux + (p_l + p_r) - (total * vel[a] + skew)
         else:
             flux = flux - (total * vel[a] + shear * jump[a])
-        out.append(0.5 * flux)
+        out.append(flux)
     loss = acoustic * enth + w2 * half_sq + skew * vel[axis]
     loss = loss + shear * (vel[t1] * jump[t1] + vel[t2] * jump[t2])
-    out.append(0.5 * (mass_l * h_l + mass_r * h_r + g * (p_l + p_r) - loss))
+    out.append(mass_l * h_l + mass_r * h_r + g * (p_l + p_r) - loss)
     return out
 
 
@@ -168,7 +168,7 @@
                     span = inner[f] - jnp.where(first, edge[f], 0.0)
                 else:
                     span = jnp.where(first, 0.0, edge[f]) - inner[f]
-                emit(f, k, row, span + after)
+                emit(f, k, row, 0.5 * (span + after))
         return carry
 
     lax.fori_loop(0, blocks, rest, 0, unroll=True)
@@ -178,7 +178,7 @@
     other = primitives(*other)
     left = [jnp.where(first, a, b) for a, b in zip(mine, other)]
     right = [jnp.where(first, b, a) for a, b in zip(mine, other)]
-    sign = jnp.where(first, 1.0, -1.0)
+    sign = jnp.where(first, 0.5, -0.5)
     return [sign * x for x in roe(left, right, 2, frame(speed_ref, 2))]
 
 
@@ -194,18 +194,15 @@
 
 
 def first_kernel(place_ref, chunk_ref, *refs):
-    sources, targets, (out_ref, near_ref, cells, faces, state_ref, sems) = refs[:6], refs[6:11], refs[11:]
-    mask_ref, link_ref, speed_ref = targets[:3]
+    sources, targets, (out_ref, near_ref, cells, faces, sems) = refs[:6], refs[6:12], refs[12:]
+    state_ref, mask_ref, link_ref, speed_ref = targets[:4]
     nj = mask_ref.shape[1]
     copies = [
         pltpu.make_async_copy(source, target, sems.at[i])
-        for i, (source, target) in enumerate(zip(sources, (state_ref, *targets)))
+        for i, (source, target) in enumerate(zip(sources, targets))
     ]
     for copy in copies:
         copy.start()
-    used = 4 * 5 * nj
-    if out_ref.shape[0] > used:
-        out_ref[used:, :] = jnp.zeros((out_ref.shape[0] - used, out_ref.shape[1]), jnp.float32)
     for copy in copies[:4]:
         copy.wait()
 
@@ -213,8 +210,7 @@
         return state_ref[f, k, pl.ds(row, 8), :]
 
     def emit(f, k, row, div):
-        out_ref[packed(f, row, k, nj), :] = load(f, k, row)
-        out_ref[packed(f, row, 2 + k, nj), :] = div
+        out_ref[f, k, pl.ds(row, 8), :] = div
 
     most_of_divergence(load, mask_ref, link_ref, speed_ref, place_ref[0] > 0, cells, faces, emit)
     near_ref[...] = cells[:LIVE, place_ref[0], PAD : PAD + nj, :]
@@ -222,17 +218,22 @@
         copy.wait()
 
 
-def first_edge_kernel(place_ref, speed_ref, near_ref, other_ref, pack_ref, out_ref):
+def first_edge_kernel(place_ref, speed_ref, near_ref, other_ref, state_ref, div_ref, out_ref):
     nj = other_ref.shape[2]
     edge = place_ref[0]
-    out_ref[...] = pack_ref[...]
+    used = 4 * 5 * nj
+    if out_ref.shape[0] > used:
+        out_ref[used:, :] = jnp.zeros((out_ref.shape[0] - used, out_ref.shape[1]), jnp.float32)
     for row in range(0, nj, 8):
-        mine = [near_ref[f, pl.ds(row, 8), :] for f in range(LIVE)]
-        other = [other_ref[f, 1 - edge, pl.ds(row, 8), :] for f in range(5)]
+        block = pl.ds(row, 8)
+        mine = [near_ref[f, block, :] for f in range(LIVE)]
+        other = [other_ref[f, 1 - edge, block, :] for f in range(5)]
         flux = outer_face(mine, other, speed_ref, edge > 0)
         for f in range(5):
-            div = packed(f, row, 2 + edge, nj)
-            out_ref[div, :] = pack_ref[div, :] + flux[f]
+            for k in range(2):
+                out_ref[packed(f, row, k, nj), :] = state_ref[f, k, block, :]
+            out_ref[packed(f, row, 2 + edge, nj), :] = div_ref[f, edge, block, :] + flux[f]
+            out_ref[packed(f, row, 3 - edge, nj), :] = div_ref[f, 1 - edge, block, :]
 
 
 def last_kernel(place_ref, speed_ref, turned_ref, mask_ref, dtau_ref, link_ref, out_ref, near_ref, cells, faces):
@@ -314,19 +315,19 @@
     return outs if len(shapes) > 1 else outs[0]
 
 
-def first_call(rows, place, chunk, field, mask, link, speed, matrix, dtau):
+def first_call(place, chunk, field, mask, link, speed, matrix, dtau):
     vmem = pl.BlockSpec(memory_space=pltpu.VMEM)
     nj, ni = mask.shape[1:]
-    given = (mask, link, speed, matrix, dtau)
-    sources = [pltpu.with_memory_space_constraint(a, pltpu.HBM) for a in (field, *given)]
+    given = (field, mask, link, speed, matrix, dtau)
+    sources = [pltpu.with_memory_space_constraint(a, pltpu.HBM) for a in given]
     outs = [pltpu.VMEM(a.shape, a.dtype) for a in given]
-    outs += [pltpu.VMEM(shape, jnp.float32) for shape in ((rows, ni), (LIVE, nj, ni))]
+    outs += [pltpu.VMEM(shape, jnp.float32) for shape in (field.shape, (LIVE, nj, ni))]
     return pl.pallas_call(
         first_kernel,
         out_shape=outs,
         in_specs=[pl.BlockSpec(memory_space=pltpu.SMEM)] * 2 + [pl.BlockSpec(memory_space=pltpu.HBM)] * 6,
-        out_specs=[vmem] * 7,
-        scratch_shapes=[*scratch(nj, ni), pltpu.VMEM(field.shape, jnp.float32), pltpu.SemaphoreType.DMA((6,))],
+        out_specs=[vmem] * 8,
+        scratch_shapes=[*scratch(nj, ni), pltpu.SemaphoreType.DMA((6,))],
         cost_estimate=pl.CostEstimate(flops=10**8, bytes_accessed=10**6, transcendentals=0),
         compiler_params=pltpu.CompilerParams(vmem_limit_bytes=24 * 2**20),
     )(place, chunk, *sources)
@@ -348,10 +349,10 @@
     with jax.named_scope("halo"):
         other = lax.ppermute(field, "span", swap)
     with jax.named_scope("first_divergence"):
-        mask, link, speed, matrix, dtau, pack, near = first_call(
-            count * 4, first, chunk, field, live_mask, link[None], frame_velocity[0], matrix, dtau
+        held, mask, link, speed, matrix, dtau, div, near = first_call(
+            first, chunk, field, live_mask, link[None], frame_velocity[0], matrix, dtau
         )
-        pack = call(first_edge_kernel, [pack.shape], (first, speed, near, other, pack), aliases={4: 0})
+        pack = call(first_edge_kernel, [(count * 4, ni)], (first, speed, near, other, held, div))
     with jax.named_scope("turn"):
         pack = turn(pack)
     with jax.named_scope("instances"):

time: 82.5 us -> 82.4 us (level)
  no operation moved by 1% of the time
where the time goes in v7:
time: 82.4 us; the launch traced here: 82.1 us
  blocking collectives  63.4 us (77%)
  starting transfers between devices  14.2 us (17%)
  Pallas kernels  4.43 us (5%)
    all_to_all x2, blocking collectives, turn(): lax.all_to_all(x.reshape(count, 4, ni), ('flap', 'gust'), 0, 0, tiled=True)  63.4 us
    ppermute x1, starting transfers between devices, shards(): other = lax.ppermute(field, 'span', swap)  8.77 us
    ppermute x1, starting transfers between devices, shards(): lax.ppermute(call(edge_kernel, [(5, nj, ni)], (first, pack)), 'span', swap)  5.41 us
    pallas_call x5, Pallas kernels, call(): pl.pallas_call(kernel, out_shape=[held(shape, jnp.float32) for shape in s...  2.6 us
    pallas_call x1, Pallas kernels, first_call(): pl.pallas_call(first_kernel, out_shape=outs, in_specs=[pl.BlockSpec(memor...  1.83 us
  transfers between devices with their start and end apart: 2, of which 1 were waited for; matrix products, arithmetic and copies ran while one was open for 0% of the time, Pallas kernels for 3%

profile of v7, /device:TPU:1, one launch (start us, length us, event | category | flops | bytes accessed | tf_op | source)
XLA Modules:
  0.0 82.1 jit_solution(6946429767625768202)
XLA Ops:
  0.0 8.8 %collective-permute-start = (f32[5,2,48,128]{3,2,1,0:T(8,128)}, f32[5,2,48,128]{3,2,1,0:T(8,128)S(1)}, u32[]{:S(2)}, u32[]{:S(2)}) collective-permute-start(f32[5,2,48,128]{3,2,1,0:T(8,128)} %bitcast.15), channel_id=1, source_target_pairs={{0,1},{1,0},{2,3},{3,2},{4,5},{5,4},{6,7},{7,6},{8,9},{9,8},{10,11... | collective-permute-start | bytes 737288 | tf_op jit(solution)/shard_map/halo/ppermute | solution.py:350
  8.8 1.8 %first_divergence.2 = (f32[5,2,48,128]{3,2,1,0:T(8,128)S(1)}, s32[2,48,128]{2,1,0:T(8,128)S(1)}, s32[1,128]{1,0:T(1,128)S(1)}, f32[1,3]{1,0:T(1,128)S(1)}, f32[2...) custom-call(s32[1]{0:T(128)} %bitcast.place_ref, ...), custom_call_target="tpu_custom_call" | custom-call | flops 100000000 | bytes 1000000 | tf_op jit(solution)/shard_map/first_divergence/pallas_call | solution.py:325
  10.6 0.0 collective-permute-done.other_ref
  10.6 0.2 first_divergence.3
  10.8 35.7 %all_to_all.10 = f32[256,4,128]{2,1,0:T(4,128)S(1)} all-to-all(f32[256,4,128]{2,1,0:T(4,128)S(1)} %bitcast.14), channel_id=1, replica_groups=mesh['flap'=16,'gust'=16,'span'=2] {'flap','gust'}, dimensions={0} | all-to-all | bytes 1048576 | tf_op jit(solution)/shard_map/turn/all_to_all | solution.py:346
  46.5 0.7 instances.1
  47.2 27.7 %all_to_all.11 = f32[256,4,128]{2,1,0:T(4,128)S(1)} all-to-all(f32[256,4,128]{2,1,0:T(4,128)S(1)} %bitcast.13), channel_id=1, replica_groups=mesh['flap'=16,'gust'=16,'span'=2] {'flap','gust'}, dimensions={0} | all-to-all | bytes 1048576 | tf_op jit(solution)/shard_map/turn_back/all_to_all | solution.py:346
  74.9 5.4 %collective-permute-start.1 = (f32[5,48,128]{2,1,0:T(8,128)S(1)}, f32[5,48,128]{2,1,0:T(8,128)S(1)}, u32[]{:S(2)}, u32[]{:S(2)}) collective-permute-start(f32[5,48,128]{2,1,0:T(8,128)S(1)} %halo.1), channel_id=1, source_target_pairs={{0,1},{1,0},{2,3},{3,2},{4,5},{5,4},{6,7},{7,6},{8,9},{9,8},{10,11... | collective-permute-start | bytes 368648 | tf_op jit(solution)/shard_map/halo/ppermute | solution.py:363
  80.3 0.9 %last_divergence.2 = (f32[5,2,48,128]{3,2,1,0:T(8,128)S(1)}, f32[7,48,128]{2,1,0:T(8,128)S(1)}) custom-call(s32[1]{0:T(128)} %bitcast.place_ref, f32[1,3]{1,0:T(1,128)S(1)} %get-tuple-element.15.speed_ref, f32[1024,128]{1,0:T(8,128)S(1)} %bitcast.11, s32[2,48,128]{2,1,0:T(8,128)S(1)} %get-tuple-element.21.mask_ref, ...), custom_call_target="tpu_custom_call" | custom-call | flops 100000000 | bytes 1000000 | tf_op jit(solution)/shard_map/last_divergence/pallas_call | solution.py:305
  81.2 0.1 collective-permute-done.1.other_ref
  81.2 0.9 %last_divergence.3 = f32[5,2,48,128]{3,2,1,0:T(8,128)} custom-call(s32[1]{0:T(128)} %bitcast.place_ref, f32[1,3]{1,0:T(1,128)S(1)} %get-tuple-element.15.speed_ref, f32[7,48,128]{2,1,0:T(8,128)S(1)} %get-tuple-element.23.near_ref, f32[5,48,128]{2,1,0:T(8,128)S(1)} %collective-permute-done.1.other_ref, f32[5,2,48,128]{3,2,1,0:T(8,128)S(1)} %get-tuple-element.24.most_ref, ...), custom_call_target="tpu_custom_call" | custom-call | bytes 1000000 | tf_op jit(solution)/shard_map/last_divergence/pallas_call | solution.py:305
  (1 shorter events, 0.0 us)
Async XLA Ops:
  0.0 10.6 %collective-permute-start = (f32[5,2,48,128]{3,2,1,0:T(8,128)}, f32[5,2,48,128]{3,2,1,0:T(8,128)S(1)}, u32[]{:S(2)}, u32[]{:S(2)}) collective-permute-start(f32[5,2,48,128]{3,2,1,0:T(8,128)} %bitcast.15), channel_id=1, source_target_pairs={{0,1},{1,0},{2,3},{3,2},{4,5},{5,4},{6,7},{7,6},{8,9},{9,8},{10,11... | collective-permute-start | bytes 737288 | tf_op jit(solution)/shard_map/halo/ppermute | solution.py:350
  74.9 6.4 %collective-permute-start.1 = (f32[5,48,128]{2,1,0:T(8,128)S(1)}, f32[5,48,128]{2,1,0:T(8,128)S(1)}, u32[]{:S(2)}, u32[]{:S(2)}) collective-permute-start(f32[5,48,128]{2,1,0:T(8,128)S(1)} %halo.1), channel_id=1, source_target_pairs={{0,1},{1,0},{2,3},{3,2},{4,5},{5,4},{6,7},{7,6},{8,9},{9,8},{10,11... | collective-permute-start | bytes 368648 | tf_op jit(solution)/shard_map/halo/ppermute | solution.py:363

commit v8 on v7

--- a/solution.py
+++ b/solution.py
@@ -12,6 +12,7 @@
 VISC = 0.12
 FLAP_OMEGA = 0.8
 GUST_OMEGA = 1.2944
+HEAD_FLAP, HEAD_GUST = 4, 10
 
 RHO, U, V, W, PR, EN, RT, LIVE = range(8)
 PAD = 8
@@ -333,17 +334,19 @@
     )(place, chunk, *sources)
 
 
-def shards(matrix, state, frame_velocity, dtau, live_mask, link):
+def shards(head, matrix, state, frame_velocity, dtau, live_mask, link):
     nj, ni = live_mask.shape[1:]
     flaps, gusts = lax.axis_size("flap"), lax.axis_size("gust")
     count = flaps * gusts
     field = state[0, 0]
     first = jnp.where(lax.axis_index("span") == 0, 1, 0).astype(jnp.int32)[None]
-    chunk = (lax.axis_index("flap") * gusts + lax.axis_index("gust")).astype(jnp.int32)[None]
+    chunk = lax.axis_index("flap") * gusts + lax.axis_index("gust")
+    chunk = jnp.where(chunk == 0, head, jnp.where(chunk == head, 0, chunk)).astype(jnp.int32)[None]
+    order = headed(count, head)
     swap = [(0, 1), (1, 0)]
 
     def turn(x):
-        y = lax.all_to_all(x.reshape(count, 4, ni), ("flap", "gust"), 0, 0, tiled=True)
+        y = lax.all_to_all(x.reshape(count, 4, ni), ("flap", "gust"), 0, 0, tiled=True, axis_index_groups=[order])
         return y.reshape(count * 4, ni)
 
     with jax.named_scope("halo"):
@@ -373,11 +376,19 @@
     return out[None, None]
 
 
+def headed(count, head):
+    order = list(range(count))
+    order[0], order[head] = head, 0
+    return order
+
+
 def solution(mesh):
     flap = instance_matrix(mesh.shape["flap"], FLAP_OMEGA)
     gust = instance_matrix(mesh.shape["gust"], GUST_OMEGA)
     matrix = np.kron(flap, np.eye(len(gust))) + np.kron(np.eye(len(flap)), gust)
-    matrix = jnp.asarray(matrix.astype(np.float32))
+    head = HEAD_FLAP * len(gust) + HEAD_GUST
+    order = headed(len(matrix), head)
+    matrix = jnp.asarray(matrix[order][:, order].astype(np.float32))
     in_specs = (
         P("flap", "gust", None, "span", None, None),
         P("flap", "gust", None),
@@ -387,5 +398,5 @@
     )
     out_specs = P("flap", "gust", None, "span", None, None)
     return jax.shard_map(
-        functools.partial(shards, matrix), mesh=mesh, in_specs=in_specs, out_specs=out_specs, check_vma=False
+        functools.partial(shards, head, matrix), mesh=mesh, in_specs=in_specs, out_specs=out_specs, check_vma=False
     )

time: 82.4 us -> 76.1 us (0.924)
  blocking collectives: 63.4 us -> 59.1 us
  starting transfers between devices: 14.2 us -> 12.2 us
    all_to_all x2, blocking collectives: 63.4 us -> 59.1 us  [turn(): lax.all_to_all(x.reshape(count, 4, ni), ('flap', 'gust'), 0, 0, tiled=Tru...]
    ppermute x1, starting transfers between devices: 5.41 us -> 3.42 us  [shards(): lax.ppermute(call(edge_kernel, [(5, nj, ni)], (first, pack)), 'span', swap)]
  transfers between devices with their start and end apart: 2 -> 2, of which waited for: 1 -> 1; matrix products, arithmetic and copies ran while one was open for 0% -> 0% of each run, Pallas kernels for 3% -> 4%
where the time goes in v8:
time: 76.1 us; the launch traced here: 75.9 us
  blocking collectives  59.1 us (78%)
  starting transfers between devices  12.2 us (16%)
  Pallas kernels  4.43 us (6%)
    all_to_all x2, blocking collectives, turn(): lax.all_to_all(x.reshape(count, 4, ni), ('flap', 'gust'), 0, 0, tiled=Tru...  59.1 us
    ppermute x1, starting transfers between devices, shards(): other = lax.ppermute(field, 'span', swap)  8.77 us
    ppermute x1, starting transfers between devices, shards(): lax.ppermute(call(edge_kernel, [(5, nj, ni)], (first, pack)), 'span', swap)  3.42 us
    pallas_call x5, Pallas kernels, call(): pl.pallas_call(kernel, out_shape=[held(shape, jnp.float32) for shape in s...  2.6 us
    pallas_call x1, Pallas kernels, first_call(): pl.pallas_call(first_kernel, out_shape=outs, in_specs=[pl.BlockSpec(memor...  1.83 us
  transfers between devices with their start and end apart: 2, of which 1 were waited for; matrix products, arithmetic and copies ran while one was open for 0% of the time, Pallas kernels for 4%

profile of v8, /device:TPU:1, one launch (start us, length us, event | category | flops | bytes accessed | tf_op | source)
XLA Modules:
  0.0 75.9 jit_solution(8542281167018044646)
XLA Ops:
  0.0 8.8 %collective-permute-start = (f32[5,2,48,128]{3,2,1,0:T(8,128)}, f32[5,2,48,128]{3,2,1,0:T(8,128)S(1)}, u32[]{:S(2)}, u32[]{:S(2)}) collective-permute-start(f32[5,2,48,128]{3,2,1,0:T(8,128)} %bitcast.15), channel_id=1, source_target_pairs={{0,1},{1,0},{2,3},{3,2},{4,5},{5,4},{6,7},{7,6},{8,9},{9,8},{10,11... | collective-permute-start | bytes 737288 | tf_op jit(solution)/shard_map/halo/ppermute | solution.py:353
  8.8 1.8 %first_divergence.2 = (f32[5,2,48,128]{3,2,1,0:T(8,128)S(1)}, s32[2,48,128]{2,1,0:T(8,128)S(1)}, s32[1,128]{1,0:T(1,128)S(1)}, f32[1,3]{1,0:T(1,128)S(1)}, f32[2...) custom-call(s32[1]{0:T(128)} %bitcast.place_ref, ...), custom_call_target="tpu_custom_call" | custom-call | flops 100000000 | bytes 1000000 | tf_op jit(solution)/shard_map/first_divergence/pallas_call | solution.py:326
  10.6 0.0 collective-permute-done.other_ref
  10.7 0.2 first_divergence.3
  10.8 30.4 %all_to_all.10 = f32[256,4,128]{2,1,0:T(4,128)S(1)} all-to-all(f32[256,4,128]{2,1,0:T(4,128)S(1)} %bitcast.14), channel_id=1, replica_groups={{148,2,4,6,8,10,12,14,16,18,20,22,24,26,28,30,32,34,36,38,40,42,44,46,4..., dimensions={0} | all-to-all | bytes 1048576 | tf_op jit(solution)/shard_map/turn/all_to_all | solution.py:349
  41.2 0.7 instances.1
  41.9 28.7 %all_to_all.11 = f32[256,4,128]{2,1,0:T(4,128)S(1)} all-to-all(f32[256,4,128]{2,1,0:T(4,128)S(1)} %bitcast.13), channel_id=1, replica_groups={{148,2,4,6,8,10,12,14,16,18,20,22,24,26,28,30,32,34,36,38,40,42,44,46,4..., dimensions={0} | all-to-all | bytes 1048576 | tf_op jit(solution)/shard_map/turn_back/all_to_all | solution.py:349
  70.6 3.4 %collective-permute-start.1 = (f32[5,48,128]{2,1,0:T(8,128)S(1)}, f32[5,48,128]{2,1,0:T(8,128)S(1)}, u32[]{:S(2)}, u32[]{:S(2)}) collective-permute-start(f32[5,48,128]{2,1,0:T(8,128)S(1)} %halo.1), channel_id=1, source_target_pairs={{0,1},{1,0},{2,3},{3,2},{4,5},{5,4},{6,7},{7,6},{8,9},{9,8},{10,11... | collective-permute-start | bytes 368648 | tf_op jit(solution)/shard_map/halo/ppermute | solution.py:366
  74.0 0.9 %last_divergence.2 = (f32[5,2,48,128]{3,2,1,0:T(8,128)S(1)}, f32[7,48,128]{2,1,0:T(8,128)S(1)}) custom-call(s32[1]{0:T(128)} %bitcast.place_ref, f32[1,3]{1,0:T(1,128)S(1)} %get-tuple-element.15.speed_ref, f32[1024,128]{1,0:T(8,128)S(1)} %bitcast.11, s32[2,48,128]{2,1,0:T(8,128)S(1)} %get-tuple-element.21.mask_ref, ...), custom_call_target="tpu_custom_call" | custom-call | flops 100000000 | bytes 1000000 | tf_op jit(solution)/shard_map/last_divergence/pallas_call | solution.py:306
  74.9 0.1 collective-permute-done.1.other_ref
  75.0 0.9 %last_divergence.3 = f32[5,2,48,128]{3,2,1,0:T(8,128)} custom-call(s32[1]{0:T(128)} %bitcast.place_ref, f32[1,3]{1,0:T(1,128)S(1)} %get-tuple-element.15.speed_ref, f32[7,48,128]{2,1,0:T(8,128)S(1)} %get-tuple-element.23.near_ref, f32[5,48,128]{2,1,0:T(8,128)S(1)} %collective-permute-done.1.other_ref, f32[5,2,48,128]{3,2,1,0:T(8,128)S(1)} %get-tuple-element.24.most_ref, ...), custom_call_target="tpu_custom_call" | custom-call | bytes 1000000 | tf_op jit(solution)/shard_map/last_divergence/pallas_call | solution.py:306
  (1 shorter events, 0.0 us)
Async XLA Ops:
  0.0 10.6 %collective-permute-start = (f32[5,2,48,128]{3,2,1,0:T(8,128)}, f32[5,2,48,128]{3,2,1,0:T(8,128)S(1)}, u32[]{:S(2)}, u32[]{:S(2)}) collective-permute-start(f32[5,2,48,128]{3,2,1,0:T(8,128)} %bitcast.15), channel_id=1, source_target_pairs={{0,1},{1,0},{2,3},{3,2},{4,5},{5,4},{6,7},{7,6},{8,9},{9,8},{10,11... | collective-permute-start | bytes 737288 | tf_op jit(solution)/shard_map/halo/ppermute | solution.py:353
  70.6 4.4 %collective-permute-start.1 = (f32[5,48,128]{2,1,0:T(8,128)S(1)}, f32[5,48,128]{2,1,0:T(8,128)S(1)}, u32[]{:S(2)}, u32[]{:S(2)}) collective-permute-start(f32[5,48,128]{2,1,0:T(8,128)S(1)} %halo.1), channel_id=1, source_target_pairs={{0,1},{1,0},{2,3},{3,2},{4,5},{5,4},{6,7},{7,6},{8,9},{9,8},{10,11... | collective-permute-start | bytes 368648 | tf_op jit(solution)/shard_map/halo/ppermute | solution.py:366

commit v9 on v8

--- a/solution.py
+++ b/solution.py
@@ -12,7 +12,7 @@
 VISC = 0.12
 FLAP_OMEGA = 0.8
 GUST_OMEGA = 1.2944
-HEAD_FLAP, HEAD_GUST = 4, 10
+HEAD_FLAP, HEAD_GUST = 12, 10
 
 RHO, U, V, W, PR, EN, RT, LIVE = range(8)
 PAD = 8

time: 76.1 us -> 76 us (level)
  no operation moved by 1% of the time
where the time goes in v9:
time: 76 us; the launch traced here: 75.8 us
  blocking collectives  59.3 us (78%)
  starting transfers between devices  11.9 us (16%)
  Pallas kernels  4.43 us (6%)
    all_to_all x2, blocking collectives, turn(): lax.all_to_all(x.reshape(count, 4, ni), ('flap', 'gust'), 0, 0, tiled=Tru...  59.3 us
    ppermute x1, starting transfers between devices, shards(): other = lax.ppermute(field, 'span', swap)  8.77 us
    ppermute x1, starting transfers between devices, shards(): lax.ppermute(call(edge_kernel, [(5, nj, ni)], (first, pack)), 'span', swap)  3.11 us
    pallas_call x5, Pallas kernels, call(): pl.pallas_call(kernel, out_shape=[held(shape, jnp.float32) for shape in s...  2.6 us
    pallas_call x1, Pallas kernels, first_call(): pl.pallas_call(first_kernel, out_shape=outs, in_specs=[pl.BlockSpec(memor...  1.83 us
  transfers between devices with their start and end apart: 2, of which 1 were waited for; matrix products, arithmetic and copies ran while one was open for 0% of the time, Pallas kernels for 4%

profile of v9, /device:TPU:1, one launch (start us, length us, event | category | flops | bytes accessed | tf_op | source)
XLA Modules:
  0.0 75.8 jit_solution(12524233206309341808)
XLA Ops:
  0.0 8.8 %collective-permute-start = (f32[5,2,48,128]{3,2,1,0:T(8,128)}, f32[5,2,48,128]{3,2,1,0:T(8,128)S(1)}, u32[]{:S(2)}, u32[]{:S(2)}) collective-permute-start(f32[5,2,48,128]{3,2,1,0:T(8,128)} %bitcast.15), channel_id=1, source_target_pairs={{0,1},{1,0},{2,3},{3,2},{4,5},{5,4},{6,7},{7,6},{8,9},{9,8},{10,11... | collective-permute-start | bytes 737288 | tf_op jit(solution)/shard_map/halo/ppermute | solution.py:353
  8.8 1.8 %first_divergence.2 = (f32[5,2,48,128]{3,2,1,0:T(8,128)S(1)}, s32[2,48,128]{2,1,0:T(8,128)S(1)}, s32[1,128]{1,0:T(1,128)S(1)}, f32[1,3]{1,0:T(1,128)S(1)}, f32[2...) custom-call(s32[1]{0:T(128)} %bitcast.place_ref, ...), custom_call_target="tpu_custom_call" | custom-call | flops 100000000 | bytes 1000000 | tf_op jit(solution)/shard_map/first_divergence/pallas_call | solution.py:326
  10.6 0.0 collective-permute-done.other_ref
  10.7 0.2 first_divergence.3
  10.8 30.5 %all_to_all.10 = f32[256,4,128]{2,1,0:T(4,128)S(1)} all-to-all(f32[256,4,128]{2,1,0:T(4,128)S(1)} %bitcast.14), channel_id=1, replica_groups={{404,2,4,6,8,10,12,14,16,18,20,22,24,26,28,30,32,34,36,38,40,42,44,46,4..., dimensions={0} | all-to-all | bytes 1048576 | tf_op jit(solution)/shard_map/turn/all_to_all | solution.py:349
  41.3 0.7 instances.1
  41.9 28.9 %all_to_all.11 = f32[256,4,128]{2,1,0:T(4,128)S(1)} all-to-all(f32[256,4,128]{2,1,0:T(4,128)S(1)} %bitcast.13), channel_id=1, replica_groups={{404,2,4,6,8,10,12,14,16,18,20,22,24,26,28,30,32,34,36,38,40,42,44,46,4..., dimensions={0} | all-to-all | bytes 1048576 | tf_op jit(solution)/shard_map/turn_back/all_to_all | solution.py:349
  70.8 3.1 %collective-permute-start.1 = (f32[5,48,128]{2,1,0:T(8,128)S(1)}, f32[5,48,128]{2,1,0:T(8,128)S(1)}, u32[]{:S(2)}, u32[]{:S(2)}) collective-permute-start(f32[5,48,128]{2,1,0:T(8,128)S(1)} %halo.1), channel_id=1, source_target_pairs={{0,1},{1,0},{2,3},{3,2},{4,5},{5,4},{6,7},{7,6},{8,9},{9,8},{10,11... | collective-permute-start | bytes 368648 | tf_op jit(solution)/shard_map/halo/ppermute | solution.py:366
  74.0 0.9 %last_divergence.2 = (f32[5,2,48,128]{3,2,1,0:T(8,128)S(1)}, f32[7,48,128]{2,1,0:T(8,128)S(1)}) custom-call(s32[1]{0:T(128)} %bitcast.place_ref, f32[1,3]{1,0:T(1,128)S(1)} %get-tuple-element.15.speed_ref, f32[1024,128]{1,0:T(8,128)S(1)} %bitcast.11, s32[2,48,128]{2,1,0:T(8,128)S(1)} %get-tuple-element.21.mask_ref, ...), custom_call_target="tpu_custom_call" | custom-call | flops 100000000 | bytes 1000000 | tf_op jit(solution)/shard_map/last_divergence/pallas_call | solution.py:306
  74.9 0.1 collective-permute-done.1.other_ref
  74.9 0.9 %last_divergence.3 = f32[5,2,48,128]{3,2,1,0:T(8,128)} custom-call(s32[1]{0:T(128)} %bitcast.place_ref, f32[1,3]{1,0:T(1,128)S(1)} %get-tuple-element.15.speed_ref, f32[7,48,128]{2,1,0:T(8,128)S(1)} %get-tuple-element.23.near_ref, f32[5,48,128]{2,1,0:T(8,128)S(1)} %collective-permute-done.1.other_ref, f32[5,2,48,128]{3,2,1,0:T(8,128)S(1)} %get-tuple-element.24.most_ref, ...), custom_call_target="tpu_custom_call" | custom-call | bytes 1000000 | tf_op jit(solution)/shard_map/last_divergence/pallas_call | solution.py:306
  (1 shorter events, 0.0 us)
Async XLA Ops:
  0.0 10.6 %collective-permute-start = (f32[5,2,48,128]{3,2,1,0:T(8,128)}, f32[5,2,48,128]{3,2,1,0:T(8,128)S(1)}, u32[]{:S(2)}, u32[]{:S(2)}) collective-permute-start(f32[5,2,48,128]{3,2,1,0:T(8,128)} %bitcast.15), channel_id=1, source_target_pairs={{0,1},{1,0},{2,3},{3,2},{4,5},{5,4},{6,7},{7,6},{8,9},{9,8},{10,11... | collective-permute-start | bytes 737288 | tf_op jit(solution)/shard_map/halo/ppermute | solution.py:353
  70.8 4.1 %collective-permute-start.1 = (f32[5,48,128]{2,1,0:T(8,128)S(1)}, f32[5,48,128]{2,1,0:T(8,128)S(1)}, u32[]{:S(2)}, u32[]{:S(2)}) collective-permute-start(f32[5,48,128]{2,1,0:T(8,128)S(1)} %halo.1), channel_id=1, source_target_pairs={{0,1},{1,0},{2,3},{3,2},{4,5},{5,4},{6,7},{7,6},{8,9},{9,8},{10,11... | collective-permute-start | bytes 368648 | tf_op jit(solution)/shard_map/halo/ppermute | solution.py:366

commit v10 on v9

--- a/solution.py
+++ b/solution.py
@@ -12,7 +12,7 @@
 VISC = 0.12
 FLAP_OMEGA = 0.8
 GUST_OMEGA = 1.2944
-HEAD_FLAP, HEAD_GUST = 12, 10
+HEAD_FLAP, HEAD_GUST = 12, 14
 
 RHO, U, V, W, PR, EN, RT, LIVE = range(8)
 PAD = 8

time: 76 us -> 76.7 us (level)
  no operation moved by 1% of the time
where the time goes in v10:
time: 76.7 us; the launch traced here: 76.4 us
  blocking collectives  59.9 us (78%)
  starting transfers between devices  12 us (16%)
  Pallas kernels  4.43 us (6%)
    all_to_all x2, blocking collectives, turn(): lax.all_to_all(x.reshape(count, 4, ni), ('flap', 'gust'), 0, 0, tiled=Tru...  59.9 us
    ppermute x1, starting transfers between devices, shards(): other = lax.ppermute(field, 'span', swap)  8.77 us
    ppermute x1, starting transfers between devices, shards(): lax.ppermute(call(edge_kernel, [(5, nj, ni)], (first, pack)), 'span', swap)  3.2 us
    pallas_call x5, Pallas kernels, call(): pl.pallas_call(kernel, out_shape=[held(shape, jnp.float32) for shape in s...  2.6 us
    pallas_call x1, Pallas kernels, first_call(): pl.pallas_call(first_kernel, out_shape=outs, in_specs=[pl.BlockSpec(memor...  1.83 us
  transfers between devices with their start and end apart: 2, of which 1 were waited for; matrix products, arithmetic and copies ran while one was open for 0% of the time, Pallas kernels for 4%

profile of v10, /device:TPU:1, one launch (start us, length us, event | category | flops | bytes accessed | tf_op | source)
XLA Modules:
  0.0 76.4 jit_solution(953916771113016854)
XLA Ops:
  0.0 8.8 %collective-permute-start = (f32[5,2,48,128]{3,2,1,0:T(8,128)}, f32[5,2,48,128]{3,2,1,0:T(8,128)S(1)}, u32[]{:S(2)}, u32[]{:S(2)}) collective-permute-start(f32[5,2,48,128]{3,2,1,0:T(8,128)} %bitcast.15), channel_id=1, source_target_pairs={{0,1},{1,0},{2,3},{3,2},{4,5},{5,4},{6,7},{7,6},{8,9},{9,8},{10,11... | collective-permute-start | bytes 737288 | tf_op jit(solution)/shard_map/halo/ppermute | solution.py:353
  8.8 1.8 %first_divergence.2 = (f32[5,2,48,128]{3,2,1,0:T(8,128)S(1)}, s32[2,48,128]{2,1,0:T(8,128)S(1)}, s32[1,128]{1,0:T(1,128)S(1)}, f32[1,3]{1,0:T(1,128)S(1)}, f32[2...) custom-call(s32[1]{0:T(128)} %bitcast.place_ref, ...), custom_call_target="tpu_custom_call" | custom-call | flops 100000000 | bytes 1000000 | tf_op jit(solution)/shard_map/first_divergence/pallas_call | solution.py:326
  10.6 0.0 collective-permute-done.other_ref
  10.7 0.2 first_divergence.3
  10.8 31.1 %all_to_all.10 = f32[256,4,128]{2,1,0:T(4,128)S(1)} all-to-all(f32[256,4,128]{2,1,0:T(4,128)S(1)} %bitcast.14), channel_id=1, replica_groups={{412,2,4,6,8,10,12,14,16,18,20,22,24,26,28,30,32,34,36,38,40,42,44,46,4..., dimensions={0} | all-to-all | bytes 1048576 | tf_op jit(solution)/shard_map/turn/all_to_all | solution.py:349
  41.9 0.7 instances.1
  42.6 28.8 %all_to_all.11 = f32[256,4,128]{2,1,0:T(4,128)S(1)} all-to-all(f32[256,4,128]{2,1,0:T(4,128)S(1)} %bitcast.13), channel_id=1, replica_groups={{412,2,4,6,8,10,12,14,16,18,20,22,24,26,28,30,32,34,36,38,40,42,44,46,4..., dimensions={0} | all-to-all | bytes 1048576 | tf_op jit(solution)/shard_map/turn_back/all_to_all | solution.py:349
  71.4 3.2 %collective-permute-start.1 = (f32[5,48,128]{2,1,0:T(8,128)S(1)}, f32[5,48,128]{2,1,0:T(8,128)S(1)}, u32[]{:S(2)}, u32[]{:S(2)}) collective-permute-start(f32[5,48,128]{2,1,0:T(8,128)S(1)} %halo.1), channel_id=1, source_target_pairs={{0,1},{1,0},{2,3},{3,2},{4,5},{5,4},{6,7},{7,6},{8,9},{9,8},{10,11... | collective-permute-start | bytes 368648 | tf_op jit(solution)/shard_map/halo/ppermute | solution.py:366
  74.6 0.9 %last_divergence.2 = (f32[5,2,48,128]{3,2,1,0:T(8,128)S(1)}, f32[7,48,128]{2,1,0:T(8,128)S(1)}) custom-call(s32[1]{0:T(128)} %bitcast.place_ref, f32[1,3]{1,0:T(1,128)S(1)} %get-tuple-element.15.speed_ref, f32[1024,128]{1,0:T(8,128)S(1)} %bitcast.11, s32[2,48,128]{2,1,0:T(8,128)S(1)} %get-tuple-element.21.mask_ref, ...), custom_call_target="tpu_custom_call" | custom-call | flops 100000000 | bytes 1000000 | tf_op jit(solution)/shard_map/last_divergence/pallas_call | solution.py:306
  75.5 0.1 collective-permute-done.1.other_ref
  75.5 0.9 %last_divergence.3 = f32[5,2,48,128]{3,2,1,0:T(8,128)} custom-call(s32[1]{0:T(128)} %bitcast.place_ref, f32[1,3]{1,0:T(1,128)S(1)} %get-tuple-element.15.speed_ref, f32[7,48,128]{2,1,0:T(8,128)S(1)} %get-tuple-element.23.near_ref, f32[5,48,128]{2,1,0:T(8,128)S(1)} %collective-permute-done.1.other_ref, f32[5,2,48,128]{3,2,1,0:T(8,128)S(1)} %get-tuple-element.24.most_ref, ...), custom_call_target="tpu_custom_call" | custom-call | bytes 1000000 | tf_op jit(solution)/shard_map/last_divergence/pallas_call | solution.py:306
  (1 shorter events, 0.0 us)
Async XLA Ops:
  0.0 10.6 %collective-permute-start = (f32[5,2,48,128]{3,2,1,0:T(8,128)}, f32[5,2,48,128]{3,2,1,0:T(8,128)S(1)}, u32[]{:S(2)}, u32[]{:S(2)}) collective-permute-start(f32[5,2,48,128]{3,2,1,0:T(8,128)} %bitcast.15), channel_id=1, source_target_pairs={{0,1},{1,0},{2,3},{3,2},{4,5},{5,4},{6,7},{7,6},{8,9},{9,8},{10,11... | collective-permute-start | bytes 737288 | tf_op jit(solution)/shard_map/halo/ppermute | solution.py:353
  71.4 4.2 %collective-permute-start.1 = (f32[5,48,128]{2,1,0:T(8,128)S(1)}, f32[5,48,128]{2,1,0:T(8,128)S(1)}, u32[]{:S(2)}, u32[]{:S(2)}) collective-permute-start(f32[5,48,128]{2,1,0:T(8,128)S(1)} %halo.1), channel_id=1, source_target_pairs={{0,1},{1,0},{2,3},{3,2},{4,5},{5,4},{6,7},{7,6},{8,9},{9,8},{10,11... | collective-permute-start | bytes 368648 | tf_op jit(solution)/shard_map/halo/ppermute | solution.py:366
